TPU v7x, 512 devices: a whole 4x8x8 slice. The times are simulated.
512 devices in a mesh: tgt: 8 (over x, y_lo), blk: 64 (over z, y_hi, core).
Axes of the slice: x: 4, y: 8 (y_hi: 4, y_lo: 2; y = y_hi * 2 + y_lo), z: 8, core: 2. Of those that a mesh axis runs over, the one named last changes fastest.
Arguments:
- queries: bfloat16 [65536, 1024], P(('tgt', 'blk')), may hold values from -184 to 184
- keys: bfloat16 [256, 1024], P('blk'), may hold values from -6.1 to 6.1
- values: bfloat16 [256, 1024], P('blk'), may hold values from -6 to 6
- out_grad: bfloat16 [65536, 1024], P(('tgt', 'blk')), may hold values from -24 to 24
Outputs:
- query_grad: bfloat16 [65536, 1024], P(('tgt', 'blk'))
- key_grad: bfloat16 [256, 1024], P('blk', 'tgt')
- value_grad: bfloat16 [256, 1024], P('blk', 'tgt')
All inputs are finite; a program needn't handle non-finite values.
Results may differ from a plain program's by a relative error of at most 0.035.
Values may be sent and summed in bfloat16 or wider, within the bound.
No kernel may reach another device: no remote copies, remote signals or barrier semaphores. Data moves between devices by JAX's collectives and lax.ppermute only.
A program may use at most 64 MiB of HBM per device.

v0:
```python
import jax
import jax.numpy as jnp
from jax import lax
from jax.sharding import PartitionSpec as P

H = 16
HD = 64


def group_grads(q_group, do_group, k_group, v_group):
    rows = q_group.shape[0]
    sources = k_group.shape[0]
    scale = HD ** (-0.5)
    q = q_group.reshape(rows, 2, HD)
    dout = do_group.reshape(rows, 2, HD)
    k = k_group.reshape(sources, 2, HD)
    v = v_group.reshape(sources, 2, HD)
    scores = jnp.einsum("rhd,shd->hrs", q, k, preferred_element_type=jnp.float32) * scale
    top = jnp.max(scores, axis=-1, keepdims=True)
    expo = jnp.exp(scores - top)
    probs = expo / jnp.sum(expo, axis=-1, keepdims=True)
    probs_low = probs.astype(jnp.bfloat16)
    output = jnp.einsum("hrs,shd->rhd", probs_low, v, preferred_element_type=jnp.float32)
    delta = jnp.transpose(jnp.sum(dout.astype(jnp.float32) * output, axis=-1))
    dprob = jnp.einsum("rhd,shd->hrs", dout, v, preferred_element_type=jnp.float32)
    dscore_low = (probs * (dprob - delta[:, :, None])).astype(jnp.bfloat16)
    dq = jnp.einsum("hrs,shd->rhd", dscore_low, k, preferred_element_type=jnp.float32) * scale
    dk = jnp.einsum("hrs,rhd->shd", dscore_low, q, preferred_element_type=jnp.float32) * scale
    dv = jnp.einsum("hrs,rhd->shd", probs_low, dout, preferred_element_type=jnp.float32)
    return (dq.reshape(rows, 2 * HD), dk.reshape(sources, 2 * HD), dv.reshape(sources, 2 * HD))


def spread_columns(summed):
    return lax.psum_scatter(
        summed.astype(jnp.bfloat16), "tgt", scatter_dimension=2, tiled=True
    ).astype(jnp.float32)


def shards(queries, keys, values, out_grad):
    keys_all, values_all = (
        lax.all_gather(keys, "blk", axis=0, tiled=True),
        lax.all_gather(values, "blk", axis=0, tiled=True),
    )
    span = 2 * HD
    dq_cols = []
    dk_cols = []
    dv_cols = []
    for group in range(H // 2):
        low = group * span
        dq, dk, dv = group_grads(
            queries[:, low : low + span],
            out_grad[:, low : low + span],
            keys_all[:, low : low + span],
            values_all[:, low : low + span],
        )
        dq_cols.append(dq)
        dk_cols.append(dk)
        dv_cols.append(dv)
    query_grad = jnp.concatenate(dq_cols, axis=1).astype(jnp.bfloat16)
    parts = jnp.stack([jnp.concatenate(dk_cols, axis=1), jnp.concatenate(dv_cols, axis=1)], axis=1)
    mine = spread_columns(lax.psum_scatter(parts, "blk", scatter_dimension=0, tiled=True))
    return (query_grad, mine[:, 0].astype(jnp.bfloat16), mine[:, 1].astype(jnp.bfloat16))


def solution(mesh):
    return jax.shard_map(
        shards,
        mesh=mesh,
        in_specs=(P(("tgt", "blk"), None), P("blk", None), P("blk", None), P(("tgt", "blk"), None)),
        out_specs=(P(("tgt", "blk"), None), P("blk", "tgt"), P("blk", "tgt")),
        check_vma=False,
    )
```

profile of v0, /device:TPU:1, one launch (start us, length us, event | category | flops | bytes accessed | tf_op | source)
XLA Modules:
  0.0 573.7 jit_solution(819577972236137441)
XLA Ops:
  7.2 0.9 fusion.91
  8.3 91.8 %all-gather.1 = bf16[64,4,1024]{2,1,0:T(4,128)(2,1)S(1)} all-gather(bf16[1,4,1024]{2,1,0:T(4,128)(2,1)} %bitcast.366), channel_id=1, replica_groups=mesh['tgt'=8,'blk'=64] {'blk'}, dimensions={0}, use_global_device_ids=true | all-gather | bytes 532480 | tf_op jit(solution)/shard_map/all_gather | solution.py:42
  100.7 77.9 %all-gather = bf16[64,4,1024]{2,1,0:T(4,128)(2,1)S(1)} all-gather(bf16[1,4,1024]{2,1,0:T(4,128)(2,1)S(1)} %bitcast.367), channel_id=1, replica_groups=mesh['tgt'=8,'blk'=64] {'blk'}, dimensions={0}, use_global_device_ids=true | all-gather | bytes 532480 | tf_op jit(solution)/shard_map/all_gather | solution.py:41
  196.5 1.7 copy.116
  198.2 1.6 copy.117
  199.9 0.9 convolution_multiply_fusion.15
  201.6 0.9 constant_dynamic-update-slice_fusion.15
  202.5 1.6 convolution_multiply_fusion.14
  204.1 1.7 copy.104
  205.7 0.9 convolution_multiply_fusion.13
  207.4 1.6 convolution_multiply_fusion.12
  209.0 1.7 copy.106
  210.7 1.6 convolution_multiply_fusion.11
  212.3 1.7 copy.107
  214.0 1.6 convolution_multiply_fusion.10
  215.6 1.7 copy.108
  217.2 1.6 convolution_multiply_fusion.9
  218.8 1.7 copy.109
  220.5 1.6 convolution_multiply_fusion.8
  222.1 1.7 copy.110
  223.8 1.0 constant_dynamic-update-slice_fusion.22
  224.7 0.9 constant_dynamic-update-slice_fusion.21
  225.7 0.9 constant_dynamic-update-slice_fusion.20
  226.6 0.9 constant_dynamic-update-slice_fusion.19
  228.6 1.4 pad_maximum_fusion
  230.0 294.8 %all-reduce.2 = bf16[256,2,1024]{2,0,1:T(8,128)(2,1)S(1)} all-reduce(f32[256,2,1024]{2,0,1:T(8,128)S(1)} %pad_maximum_fusion), channel_id=2, replica_groups=mesh['tgt'=8,'blk'=64] {'blk'}, use_global_device_ids=true, to_apply=%region_24.0.clone | all-reduce | flops 524288 | bytes 3145728
  524.8 1.4 dynamic-slice
  527.4 0.9 reshape.270
  528.4 1.1 fusion.48
  529.4 1.1 fusion.49
  532.8 31.8 %reduce-scatter.5.cloned.1.call-done = bf16[128,8]{1,0:T(8,128)(2,1)} async-done(((bf16[1024,8]{1,0:T(8,128)(2,1)}), bf16[128,8]{1,0:T(8,128)(2,1)}) %reduce-scatter.5.cloned.1.call-update) | async-done | bytes 2064
  564.6 0.8 reshape.271
  (205 shorter events, 24.7 us)
Async XLA Ops:
  7.2 93.3 %copy-start.37 = (bf16[128,1024]{1,0:T(8,128)(2,1)S(1)}, bf16[128,1024]{1,0:T(8,128)(2,1)}, u32[]{:S(2)}) copy-start(bf16[128,1024]{1,0:T(8,128)(2,1)} %param.4) | copy-start | bytes 786436
  7.2 93.5 %copy-start.38 = (bf16[4,1024]{1,0:T(4,128)(2,1)S(1)}, bf16[4,1024]{1,0:T(4,128)(2,1)}, u32[]{:S(2)}) copy-start(bf16[4,1024]{1,0:T(4,128)(2,1)} %param.5) | copy-start | bytes 24580
  7.2 557.4 %reduce-scatter.5.cloned.1.call-start = ((), (), s32[]{:S(2)}) async-start(), calls=%async_computation.1 | async-start | bytes 294912
  100.6 79.4 %copy-start.29 = (bf16[128,128]{0,1:T(8,128)(2,1)}, bf16[128,128]{0,1:T(8,128)(2,1)S(1)}, u32[]{:S(2)}) copy-start(bf16[128,128]{0,1:T(8,128)(2,1)S(1)} %copy.63) | copy-start | bytes 98308
  180.0 19.9 %copy-start.5 = (bf16[2,128,256]{2,1,0:T(8,128)(2,1)}, bf16[2,128,256]{2,1,0:T(8,128)(2,1)S(1)}, u32[]{:S(2)}) copy-start(bf16[2,128,256]{2,1,0:T(8,128)(2,1)S(1)} %fusion.32) | copy-start | bytes 393220
  181.6 20.9 %copy-start.6 = (bf16[2,128,256]{2,1,0:T(8,128)(2,1)}, bf16[2,128,256]{2,1,0:T(8,128)(2,1)S(1)}, u32[]{:S(2)}) copy-start(bf16[2,128,256]{2,1,0:T(8,128)(2,1)S(1)} %fusion.33) | copy-start | bytes 393220
  183.3 22.5 %copy-start.7 = (bf16[2,128,256]{2,1,0:T(8,128)(2,1)}, bf16[2,128,256]{2,1,0:T(8,128)(2,1)S(1)}, u32[]{:S(2)}) copy-start(bf16[2,128,256]{2,1,0:T(8,128)(2,1)S(1)} %fusion.34) | copy-start | bytes 393220
  184.9 22.5 %copy-start.9 = (bf16[2,128,256]{2,1,0:T(8,128)(2,1)}, bf16[2,128,256]{2,1,0:T(8,128)(2,1)S(1)}, u32[]{:S(2)}) copy-start(bf16[2,128,256]{2,1,0:T(8,128)(2,1)S(1)} %fusion.35) | copy-start | bytes 393220
  186.5 24.2 %copy-start.11 = (bf16[2,128,256]{2,1,0:T(8,128)(2,1)}, bf16[2,128,256]{2,1,0:T(8,128)(2,1)S(1)}, u32[]{:S(2)}) copy-start(bf16[2,128,256]{2,1,0:T(8,128)(2,1)S(1)} %fusion.36) | copy-start | bytes 393220
  188.8 25.2 %copy-start.13 = (bf16[2,128,256]{2,1,0:T(8,128)(2,1)}, bf16[2,128,256]{2,1,0:T(8,128)(2,1)S(1)}, u32[]{:S(2)}) copy-start(bf16[2,128,256]{2,1,0:T(8,128)(2,1)S(1)} %fusion.37) | copy-start | bytes 393220
  189.3 4.1 copy-start.1
  191.1 26.2 %copy-start.15 = (bf16[2,128,256]{2,1,0:T(8,128)(2,1)}, bf16[2,128,256]{2,1,0:T(8,128)(2,1)S(1)}, u32[]{:S(2)}) copy-start(bf16[2,128,256]{2,1,0:T(8,128)(2,1)S(1)} %fusion.38) | copy-start | bytes 393220
  191.6 6.6 %copy-start.3 = (bf16[256,128]{0,1:T(8,128)(2,1)}, bf16[256,128]{0,1:T(8,128)(2,1)S(1)}, u32[]{:S(2)}) copy-start(bf16[256,128]{0,1:T(8,128)(2,1)S(1)} %copy.137) | copy-start | bytes 196612
  193.4 27.1 %copy-start.17 = (bf16[2,128,256]{2,1,0:T(8,128)(2,1)}, bf16[2,128,256]{2,1,0:T(8,128)(2,1)S(1)}, u32[]{:S(2)}) copy-start(bf16[2,128,256]{2,1,0:T(8,128)(2,1)S(1)} %fusion.39) | copy-start | bytes 393220
  193.4 6.4 %copy-start.28 = (f32[2,256,64]{1,2,0:T(8,128)S(1)}, f32[2,256,64]{1,2,0:T(8,128)}, u32[]{:S(2)}) copy-start(f32[2,256,64]{1,2,0:T(8,128)} %fusion.108) | copy-start | bytes 393220
  206.7 20.8 %copy-start.20 = (f32[256,128]{1,0:T(8,128)S(1)}, f32[256,128]{1,0:T(8,128)}, u32[]{:S(2)}) copy-start(f32[256,128]{1,0:T(8,128)} %copy.116) | copy-start | bytes 393220
  207.4 20.1 %copy-start.19 = (f32[256,128]{1,0:T(8,128)S(1)}, f32[256,128]{1,0:T(8,128)}, u32[]{:S(2)}) copy-start(f32[256,128]{1,0:T(8,128)} %copy.117) | copy-start | bytes 393220
  210.7 16.9 %copy-start.21 = (f32[256,128]{1,0:T(8,128)S(1)}, f32[256,128]{1,0:T(8,128)}, u32[]{:S(2)}) copy-start(f32[256,128]{1,0:T(8,128)} %copy.104) | copy-start | bytes 393220
  212.3 15.3 %copy-start.22 = (f32[256,128]{1,0:T(8,128)S(1)}, f32[256,128]{1,0:T(8,128)}, u32[]{:S(2)}) copy-start(f32[256,128]{1,0:T(8,128)} %copy.105) | copy-start | bytes 393220
  215.6 12.1 %copy-start.23 = (f32[256,128]{1,0:T(8,128)S(1)}, f32[256,128]{1,0:T(8,128)}, u32[]{:S(2)}) copy-start(f32[256,128]{1,0:T(8,128)} %copy.106) | copy-start | bytes 393220
  218.8 8.9 %copy-start.24 = (f32[256,128]{1,0:T(8,128)S(1)}, f32[256,128]{1,0:T(8,128)}, u32[]{:S(2)}) copy-start(f32[256,128]{1,0:T(8,128)} %copy.107) | copy-start | bytes 393220
  222.1 5.6 copy-start.25
  223.8 4.0 copy-start.27
  524.8 5.8 %copy-start.8 = (bf16[2,128,256]{2,1,0:T(8,128)(2,1)S(1)}, bf16[2,128,256]{2,1,0:T(8,128)(2,1)}, u32[]{:S(2)}) copy-start(bf16[2,128,256]{2,1,0:T(8,128)(2,1)} %copy-done.7) | copy-start | bytes 393220
  524.8 5.9 %copy-start.10 = (bf16[2,128,256]{2,1,0:T(8,128)(2,1)S(1)}, bf16[2,128,256]{2,1,0:T(8,128)(2,1)}, u32[]{:S(2)}) copy-start(bf16[2,128,256]{2,1,0:T(8,128)(2,1)} %copy-done.9) | copy-start | bytes 393220
  524.8 6.1 %copy-start.12 = (bf16[2,128,256]{2,1,0:T(8,128)(2,1)S(1)}, bf16[2,128,256]{2,1,0:T(8,128)(2,1)}, u32[]{:S(2)}) copy-start(bf16[2,128,256]{2,1,0:T(8,128)(2,1)} %copy-done.11) | copy-start | bytes 393220
  524.8 6.3 %copy-start.14 = (bf16[2,128,256]{2,1,0:T(8,128)(2,1)S(1)}, bf16[2,128,256]{2,1,0:T(8,128)(2,1)}, u32[]{:S(2)}) copy-start(bf16[2,128,256]{2,1,0:T(8,128)(2,1)} %copy-done.13) | copy-start | bytes 393220
  524.8 6.5 %copy-start.2 = (bf16[256,128]{0,1:T(8,128)(2,1)S(1)}, bf16[256,128]{0,1:T(8,128)(2,1)}, u32[]{:S(2)}) copy-start(bf16[256,128]{0,1:T(8,128)(2,1)} %copy-done.1) | copy-start | bytes 196612
  524.8 6.5 %copy-start.16 = (bf16[2,128,256]{2,1,0:T(8,128)(2,1)S(1)}, bf16[2,128,256]{2,1,0:T(8,128)(2,1)}, u32[]{:S(2)}) copy-start(bf16[2,128,256]{2,1,0:T(8,128)(2,1)} %copy-done.15) | copy-start | bytes 393220
  524.8 6.6 %copy-start.4 = (bf16[256,128]{0,1:T(8,128)(2,1)S(1)}, bf16[256,128]{0,1:T(8,128)(2,1)}, u32[]{:S(2)}) copy-start(bf16[256,128]{0,1:T(8,128)(2,1)} %copy-done.3) | copy-start | bytes 196612
  524.8 6.6 %copy-start.18 = (bf16[2,128,256]{2,1,0:T(8,128)(2,1)S(1)}, bf16[2,128,256]{2,1,0:T(8,128)(2,1)}, u32[]{:S(2)}) copy-start(bf16[2,128,256]{2,1,0:T(8,128)(2,1)} %copy-done.17) | copy-start | bytes 393220
  532.8 34.1 %copy-start.39 = (bf16[128,1024]{1,0:T(8,128)(2,1)}, bf16[128,1024]{1,0:T(8,128)(2,1)S(1)}, u32[]{:S(2)}) copy-start(bf16[128,1024]{1,0:T(8,128)(2,1)S(1)} %constant_dynamic-update-slice_fusion) | copy-start | bytes 786436
  (9 other events, 22.4 us)
Sparse Core Ops, SparseCore 0:
  528.5 36.0 reduce-scatter.4
where the time goes:
time: 579 us; the launch traced here: 574 us
  blocking collectives  464 us (80%)
  local copies, waits for them, and re-layouts  34.8 us (6%)
  waiting for transfers between devices  31.8 us (5%)
  matrix products  24.4 us (4%)
  between operations  15.9 us (3%)
    unnamed x1, blocking collectives  295 us
    all_gather x1, blocking collectives, shards(): lax.all_gather(values, 'blk', axis=0, tiled=True)  91.8 us
    all_gather x1, blocking collectives, shards(): lax.all_gather(keys, 'blk', axis=0, tiled=True)  77.9 us
    unnamed x2, waiting for transfers between devices  31.8 us
    unnamed x125, local copies, waits for them, and re-layouts  12.8 us
  transfers between devices with their start and end apart: 1, of which 1 were waited for; matrix products, arithmetic and copies ran while one was open for 1% of the time, Pallas kernels for 0%

commit v1 on v0

v1 whole, which is shorter than its diff:
```python
import jax
import jax.numpy as jnp
from jax import lax
from jax.experimental import pallas as pl
from jax.experimental.pallas import tpu as pltpu
from jax.sharding import Mesh, PartitionSpec as P

HD = 64
PAIR = 2 * HD
SCALE = HD ** (-0.5)
LOG2E = 1.4426950408889634
BF16 = jnp.bfloat16
F32 = jnp.float32
OTHER = [(0, 1), (1, 0)]
SOURCE_AXES = ("z", "yhi")


def matmul(a, b):
    return lax.dot_general(a, b, (((1,), (0,)), ((), ())), preferred_element_type=F32)


def matmul_bt(a, b):
    return lax.dot_general(a, b, (((1,), (1,)), ((), ())), preferred_element_type=F32)


def split_heads(a, axis):
    first = lax.broadcasted_iota(jnp.int32, a.shape, 1) < HD
    zero = jnp.zeros_like(a)
    return jnp.concatenate([jnp.where(first, a, zero), jnp.where(first, zero, a)], axis=axis)


def attention_kernel(near_ref, far_ref, kv_ref, dq_near_ref, dq_far_ref, dkv_ref, p_ref, ds_ref):
    sources = kv_ref.shape[0]
    width = kv_ref.shape[1] // 2
    rows = near_ref.shape[2]
    blocks = [(near_ref, dq_near_ref, 0), (near_ref, dq_near_ref, 1), (far_ref, dq_far_ref, 0), (far_ref, dq_far_ref, 1)]
    for low in range(0, width, PAIR):
        cols = slice(low, low + PAIR)
        k = kv_ref[:, cols]
        k2 = split_heads(k, 0)
        v2 = split_heads(kv_ref[:, width + low : width + low + PAIR], 0)
        k2t = k2.T
        for at, (ref, dq_ref, part) in enumerate(blocks):
            span = slice(at * rows, (at + 1) * rows)
            score = matmul_bt(k2, ref[part, 0, :, cols]) * (SCALE * LOG2E)
            dprob = matmul_bt(v2, ref[part, 1, :, cols])
            score = score.reshape(2, sources, rows)
            dprob = dprob.reshape(2, sources, rows)
            expo = jnp.exp2(score - jnp.max(score, axis=1, keepdims=True))
            probs = expo * (1.0 / jnp.sum(expo, axis=1, keepdims=True))
            p_low = probs.astype(BF16)
            delta = jnp.sum(p_low.astype(F32) * dprob, axis=1, keepdims=True)
            ds_low = (probs * (dprob - delta)).astype(BF16)
            p_ref[:, :, span] = p_low
            ds_ref[:, :, span] = ds_low
            dq_t = matmul(k2t, ds_low.reshape(2 * sources, rows)) * SCALE
            dq_ref[part, :, cols] = dq_t.T.astype(BF16)
        q = jnp.concatenate([ref[part, 0, :, cols] for ref, _, part in blocks], axis=0)
        do = jnp.concatenate([ref[part, 1, :, cols] for ref, _, part in blocks], axis=0)
        dk = matmul(jnp.concatenate([ds_ref[0], ds_ref[1]], axis=1), split_heads(q, 0)) * SCALE
        dv = matmul(jnp.concatenate([p_ref[0], p_ref[1]], axis=1), split_heads(do, 0))
        dkv_ref[:, cols] = dk.astype(BF16)
        dkv_ref[:, width + low : width + low + PAIR] = dv.astype(BF16)


def attention(near, far, kv):
    _, _, rows, width = near.shape
    sources = kv.shape[0]
    vmem = pl.BlockSpec(memory_space=pltpu.VMEM)
    pairs = 2 * 2 * rows * sources * width // HD
    return pl.pallas_call(
        attention_kernel,
        out_shape=(
            jax.ShapeDtypeStruct((2, rows, width), BF16),
            jax.ShapeDtypeStruct((2, rows, width), BF16),
            jax.ShapeDtypeStruct((sources, 2 * width), BF16),
        ),
        in_specs=[vmem] * 3,
        out_specs=(vmem, vmem, vmem),
        scratch_shapes=[
            pltpu.VMEM((2, sources, 4 * rows), BF16),
            pltpu.VMEM((2, sources, 4 * rows), BF16),
        ],
        compiler_params=pltpu.CompilerParams(vmem_limit_bytes=32 * 1024 * 1024),
        cost_estimate=pl.CostEstimate(flops=20 * pairs * HD, bytes_accessed=2 * 1024 * 1024, transcendentals=pairs),
    )(near, far, kv)


def pick(flag, a, b):
    return jnp.where(flag, a, b)


def shards(queries, keys, values, out_grad):
    rows, model = queries.shape
    held = keys.shape[0]
    half = model // 2
    core = lax.axis_index("core") == 0
    side = lax.axis_index("ylo") == 0
    chips = lax.axis_size(SOURCE_AXES)
    xs = lax.axis_size("x")

    packed = jnp.concatenate([queries, out_grad, keys, values], axis=0)
    kept = pick(core, packed[:, :half], packed[:, half:])
    moved = lax.ppermute(pick(core, packed[:, half:], packed[:, :half]), "core", OTHER)

    def source_rows(low):
        a, b = kept[low : low + held], moved[low : low + held]
        both = pick(core, jnp.concatenate([a, b], axis=0), jnp.concatenate([b, a], axis=0))
        both = both.reshape(2 * held, half // (2 * PAIR), 2, PAIR)
        return pick(side, both[:, :, 0], both[:, :, 1]).reshape(2 * held, half // 2)

    block = jnp.concatenate([source_rows(2 * rows), source_rows(2 * rows + held)], axis=1)

    targets = jnp.stack([kept[: 2 * rows], moved[: 2 * rows]])
    targets = targets.reshape(2, 2, rows, half // (2 * PAIR), 2, PAIR)
    one, two = targets[:, :, :, :, 0], targets[:, :, :, :, 1]
    shape = (2, 2, rows, half // 2)
    near = pick(side, one, two).reshape(shape)
    far = lax.ppermute(pick(side, two, one).reshape(shape), "ylo", OTHER)

    kv = lax.all_to_all(jnp.broadcast_to(block, (chips,) + block.shape), SOURCE_AXES, 0, 0, tiled=True)
    dq_near, dq_far, dkv = attention(near, far, kv.reshape(chips * 2 * held, half))

    dq_back = lax.ppermute(dq_far, "ylo", OTHER)
    parts = (2, rows, half // (2 * PAIR), 1, PAIR)
    a, b = dq_near.reshape(parts), dq_back.reshape(parts)
    dq = jnp.concatenate([pick(side, a, b), pick(side, b, a)], axis=3).reshape(2, rows, half)
    dq_home = lax.ppermute(dq[1], "core", OTHER)
    query_grad = jnp.concatenate([pick(core, dq[0], dq_home), pick(core, dq_home, dq[0])], axis=1)

    parts = lax.all_to_all(dkv.reshape(chips, 2 * held, half), SOURCE_AXES, 0, 0, tiled=True)
    total = jnp.sum(parts.astype(F32), axis=0).reshape(2, held, 2, half // (2 * PAIR), PAIR)
    total = jnp.transpose(total, (3, 0, 1, 2, 4)).reshape(xs // 2, 2, held, 2 * PAIR)
    none = jnp.zeros_like(total)
    outgoing = jnp.concatenate([pick(core, total, none), pick(core, none, total)], axis=0)
    mine = lax.all_to_all(outgoing.reshape(2 * xs, held, 2 * PAIR), ("x", "core"), 0, 0, tiled=True)
    mine = jnp.sum(mine, axis=0)
    return query_grad, mine[:, :PAIR].astype(BF16), mine[:, PAIR:].astype(BF16)


def solution(mesh):
    fine = Mesh(mesh.devices.reshape(4, 2, 8, 4, 2), ("x", "ylo", "z", "yhi", "core"))
    targets = ("x", "ylo", "z", "yhi", "core")
    sources = ("z", "yhi", "core")
    return jax.shard_map(
        shards,
        mesh=fine,
        in_specs=(P(targets, None), P(sources, None), P(sources, None), P(targets, None)),
        out_specs=(P(targets, None), P(sources, ("x", "ylo")), P(sources, ("x", "ylo"))),
        check_vma=False,
    )
```

time: 579 us -> 79.5 us (0.14)
  blocking collectives: 464 us -> 0 us
  starting transfers between devices: 0.04 us -> 46.6 us
  local copies, waits for them, and re-layouts: 34.8 us -> 3.15 us
  matrix products: 24.4 us -> 0 us
  between operations: 15.9 us -> 0.91 us
  waiting for transfers between devices: 31.8 us -> 21.1 us
    unnamed x1 -> x0, blocking collectives: 295 us -> none
    all_gather x2 -> x0, blocking collectives: 170 us -> none  [the longest x1 91.8 us: shards(): lax.all_gather(values, 'blk', axis=0, tiled=True)]
    unnamed x2 -> x0, waiting for transfers between devices: 31.8 us -> none
    all_to_all x0 -> x3, starting transfers between devices: none -> 28.7 us  [the longest x1 10.5 us: shards(): lax.all_to_all(dkv.reshape(chips, 2 * held, half), SOURCE_AXES, 0, 0, til...]
    dot_general x40 -> x0, matrix products: 21 us -> none  [the longest x8 11.3 us: group_grads(): jnp.einsum('hrs,rhd->shd', dscore_low, q, preferred_element_type=jnp.floa...]
    reshape x24 -> x0, local copies, waits for them, and re-layouts: 19 us -> none  [the longest x8 11.5 us: group_grads(): dk.reshape(sources, 2 * HD)]
    ppermute x0 -> x4, starting transfers between devices: none -> 17.8 us  [the longest x1 8.79 us: shards(): lax.ppermute(pick(core, packed[:, half:], packed[:, :half]), 'core', OTHER)]
    unnamed x125 -> x2, local copies, waits for them, and re-layouts: 12.8 us -> 0.23 us
  transfers between devices with their start and end apart: 1 -> 7, of which waited for: 1 -> 5; matrix products, arithmetic and copies ran while one was open for 1% -> 4% of each run, Pallas kernels for 0% -> 0%
where the time goes in v1:
time: 79.5 us; the launch traced here: 79 us
  starting transfers between devices  46.6 us (59%)
  waiting for transfers between devices  21.1 us (27%)
  Pallas kernels  4.23 us (5%)
  local copies, waits for them, and re-layouts  3.15 us (4%)
  other arithmetic  3.06 us (4%)
  between operations  0.91 us (1%)
    all_to_all x1, starting transfers between devices, shards(): lax.all_to_all(dkv.reshape(chips, 2 * held, half), SOURCE_AXES, 0, 0, til...  10.5 us
    all_to_all x1, starting transfers between devices, shards(): lax.all_to_all(jnp.broadcast_to(block, (chips,) + block.shape), SOURCE_AX...  10.3 us
    ppermute x1, waiting for transfers between devices, shards(): far = lax.ppermute(pick(side, two, one).reshape(shape), 'ylo', OTHER)  9.22 us
    ppermute x1, starting transfers between devices, shards(): lax.ppermute(pick(core, packed[:, half:], packed[:, :half]), 'core', OTHER)  8.79 us
    all_to_all x1, starting transfers between devices, shards(): lax.all_to_all(outgoing.reshape(2 * xs, held, 2 * PAIR), ('x', 'core'), 0...  7.9 us
    all_to_all x1, waiting for transfers between devices, shards(): lax.all_to_all(dkv.reshape(chips, 2 * held, half), SOURCE_AXES, 0, 0, til...  6.26 us
    pallas_call x1, Pallas kernels, attention(): pl.pallas_call(attention_kernel, out_shape=(jax.ShapeDtypeStruct((2, rows...  4.23 us
    all_to_all x1, waiting for transfers between devices, shards(): lax.all_to_all(outgoing.reshape(2 * xs, held, 2 * PAIR), ('x', 'core'), 0...  3.99 us
  transfers between devices with their start and end apart: 7, of which 5 were waited for; matrix products, arithmetic and copies ran while one was open for 4% of the time, Pallas kernels for 0%

profile of v1, /device:TPU:1, one launch (start us, length us, event | category | flops | bytes accessed | tf_op | source)
XLA Modules:
  0.0 79.0 jit_solution(8793249615301805752)
XLA Ops:
  0.6 1.1 %pad_maximum_fusion = bf16[264,1024]{1,0:T(8,128)(2,1)S(1)} fusion(bf16[4,1024]{1,0:T(4,128)(2,1)} %param.6, bf16[4,1024]{1,0:T(4,128)(2,1)} %param.5, bf16[128,1024]{1,0:T(8,128)(2,1)} %param.7, bf16[128,1024]{1,0:T(8,128)(2,1)} %param.4), kind=kLoop, calls=%fused_computation | loop fusion | flops 2162688 | bytes 1081344 | tf_op jit(solution)/shard_map/concatenate | solution.py:102
  1.8 8.8 %collective-permute-start = (bf16[264,512]{1,0:T(8,128)(2,1)S(1)}, bf16[264,512]{1,0:T(8,128)(2,1)S(1)}, u32[]{:S(2)}, u32[]{:S(2)}) collective-permute-start(bf16[264,512]{1,0:T(8,128)(2,1)S(1)} %get-tuple-element.9), channel_id=1, source_target_pairs={{0,1},{1,0},{2,3},{3,2},{4,5},{5,4},{6,7},{7,6},{8,9},{9,8},{10,11... | collective-permute-start | bytes 811016 | tf_op jit(solution)/shard_map/ppermute | solution.py:104
  10.6 0.1 stack.9
  10.7 0.1 copy_dynamic-update-slice_fusion.1
  10.9 0.9 %collective-permute-done = bf16[264,512]{1,0:T(8,128)(2,1)S(1)} collective-permute-done((bf16[264,512]{1,0:T(8,128)(2,1)S(1)}, bf16[264,512]{1,0:T(8,128)(2,1)S(1)}, u32[]{:S(2)}, u32[]{:S(2)}) %collective-permute-start) | collective-permute-done | bytes 270368 | tf_op jit(solution)/shard_map/ppermute | solution.py:104
  11.8 0.1 stack.10
  11.9 0.7 broadcast_in_dim.6
  12.6 10.3 %all-to-all-start = ((bf16[32,8,512]{2,1,0:T(8,128)(2,1)}), bf16[32,8,512]{2,1,0:T(8,128)(2,1)S(1)}, u32[]{:S(2)}, u32[]{:S(2)}) async-start(bf16[32,8,512]{2,1,0:T(8,128)(2,1)} %broadcast_in_dim.6), calls=%async_computation | async-start | bytes 524288 | tf_op jit(solution)/shard_map/all_to_all | solution.py:121
  23.0 0.2 copy_dynamic-update-slice_fusion
  23.1 0.4 broadcast_select_fusion
  23.6 0.2 select_n.151
  23.7 2.3 %collective-permute-start.1 = (bf16[2,2,128,256]{3,2,1,0:T(8,128)(2,1)S(1)}, bf16[2,2,128,256]{3,2,1,0:T(8,128)(2,1)S(1)}, u32[]{:S(2)}, u32[]{:S(2)}) collective-permute-start(bf16[2,2,128,256]{3,2,1,0:T(8,128)(2,1)S(1)} %select_n.151), channel_id=1, source_target_pairs={{0,64},{64,0},{1,65},{65,1},{2,66},{66,2},{3,67},{67,3},{4,68},{68... | collective-permute-start | bytes 786440 | tf_op jit(solution)/shard_map/ppermute | solution.py:119
  26.0 0.2 select_n.149.near_ref
  26.2 9.2 %collective-permute-done.1.far_ref = bf16[2,2,128,256]{3,2,1,0:T(8,128)(2,1)S(1)} collective-permute-done((bf16[2,2,128,256]{3,2,1,0:T(8,128)(2,1)S(1)}, bf16[2,2,128,256]{3,2,1,0:T(8,128)(2,1)S(1)}, u32[]{:S(2)}, u32[]{:S(2)}) %collective-permute-start.1) | collective-permute-done | bytes 262176 | tf_op jit(solution)/shard_map/ppermute | solution.py:119
  35.4 4.2 %shard_map.67 = (bf16[2,128,256]{2,1,0:T(8,128)(2,1)S(1)}, bf16[2,128,256]{2,1,0:T(8,128)(2,1)S(1)}, bf16[256,512]{1,0:T(8,128)(2,1)}) custom-call(bf16[2,2,128,256]{3,2,1,0:T(8,128)(2,1)S(1)} %select_n.149.near_ref, bf16[2,2,128,256]{3,2,1,0:T(8,128)(2,1)S(1)} %collective-permute-done.1.far_ref, bf16[256,512]{1,0:T(8,128)(2,1)S(1)} %bitcast.23), custom_call_target="tpu_custom_call" | custom-call | flops 671088640 | bytes 2097152 | tf_op jit(solution)/shard_map/pallas_call | solution.py:71
  39.7 3.1 %collective-permute-start.2 = (bf16[2,128,256]{2,1,0:T(8,128)(2,1)S(1)}, bf16[2,128,256]{2,1,0:T(8,128)(2,1)S(1)}, u32[]{:S(2)}, u32[]{:S(2)}) collective-permute-start(bf16[2,128,256]{2,1,0:T(8,128)(2,1)S(1)} %get-tuple-element.7), channel_id=1, source_target_pairs={{0,64},{64,0},{1,65},{65,1},{2,66},{66,2},{3,67},{67,3},{4,68},{68... | collective-permute-start | bytes 393224 | tf_op jit(solution)/shard_map/ppermute | solution.py:124
  42.8 10.5 %all-to-all-start.1 = ((bf16[32,8,512]{2,1,0:T(8,128)(2,1)}), bf16[32,8,512]{2,1,0:T(8,128)(2,1)S(1)}, u32[]{:S(2)}, u32[]{:S(2)}) async-start(bf16[32,8,512]{2,1,0:T(8,128)(2,1)} %bitcast.7), calls=%async_computation.1 | async-start | bytes 524288 | tf_op jit(solution)/shard_map/all_to_all | solution.py:131
  53.4 0.1 constant_dynamic-update-slice_fusion.1
  53.5 0.1 constant_dynamic-update-slice_fusion
  53.6 0.2 fusion.4
  53.8 0.2 copy.18
  54.0 0.1 squeeze.5
  54.1 3.7 %collective-permute-start.3 = (bf16[128,512]{1,0:T(8,128)(2,1)S(1)}, bf16[128,512]{1,0:T(8,128)(2,1)S(1)}, u32[]{:S(2)}, u32[]{:S(2)}) collective-permute-start(bf16[128,512]{1,0:T(8,128)(2,1)S(1)} %squeeze.5), channel_id=1, source_target_pairs={{0,1},{1,0},{2,3},{3,2},{4,5},{5,4},{6,7},{7,6},{8,9},{9,8},{10,11... | collective-permute-start | bytes 393224 | tf_op jit(solution)/shard_map/ppermute | solution.py:128
  57.8 0.2 copy.17
  58.0 0.1 squeeze.4
  58.0 0.7 collective-permute-done.3
  58.7 6.3 %all-to-all-done.1 = bf16[32,8,512]{2,1,0:T(8,128)(2,1)S(1)} async-done(((bf16[32,8,512]{2,1,0:T(8,128)(2,1)}), bf16[32,8,512]{2,1,0:T(8,128)(2,1)S(1)}, u32[]{:S(2)}, u32[]{:S(2)}) %all-to-all-start.1) | async-done | bytes 262176 | tf_op jit(solution)/shard_map/all_to_all | solution.py:131
  65.1 0.6 pad_maximum_fusion.2
  65.7 7.9 %all-to-all-start.2 = ((f32[8,4,256]{2,1,0:T(4,128)}), f32[8,4,256]{2,1,0:T(4,128)S(1)}, u32[]{:S(2)}, u32[]{:S(2)}) async-start(f32[8,4,256]{2,1,0:T(4,128)} %bitcast.12), calls=%async_computation.2 | async-start | bytes 65536 | tf_op jit(solution)/shard_map/all_to_all | solution.py:136
  73.6 0.7 pad_maximum_fusion.1
  74.4 4.0 %all-to-all-done.2 = f32[8,4,256]{2,1,0:T(4,128)S(1)} async-done(((f32[8,4,256]{2,1,0:T(4,128)}), f32[8,4,256]{2,1,0:T(4,128)S(1)}, u32[]{:S(2)}, u32[]{:S(2)}) %all-to-all-start.2) | async-done | bytes 32800 | tf_op jit(solution)/shard_map/all_to_all | solution.py:136
  78.4 0.6 fusion.5
  (22 shorter events, 0.4 us)
Async XLA Ops:
  1.8 9.9 %collective-permute-start = (bf16[264,512]{1,0:T(8,128)(2,1)S(1)}, bf16[264,512]{1,0:T(8,128)(2,1)S(1)}, u32[]{:S(2)}, u32[]{:S(2)}) collective-permute-start(bf16[264,512]{1,0:T(8,128)(2,1)S(1)} %get-tuple-element.9), channel_id=1, source_target_pairs={{0,1},{1,0},{2,3},{3,2},{4,5},{5,4},{6,7},{7,6},{8,9},{9,8},{10,11... | collective-permute-start | bytes 811016 | tf_op jit(solution)/shard_map/ppermute | solution.py:104
  12.6 22.8 %all-to-all-start = ((bf16[32,8,512]{2,1,0:T(8,128)(2,1)}), bf16[32,8,512]{2,1,0:T(8,128)(2,1)S(1)}, u32[]{:S(2)}, u32[]{:S(2)}) async-start(bf16[32,8,512]{2,1,0:T(8,128)(2,1)} %broadcast_in_dim.6), calls=%async_computation | async-start | bytes 524288 | tf_op jit(solution)/shard_map/all_to_all | solution.py:121
  23.7 11.7 %collective-permute-start.1 = (bf16[2,2,128,256]{3,2,1,0:T(8,128)(2,1)S(1)}, bf16[2,2,128,256]{3,2,1,0:T(8,128)(2,1)S(1)}, u32[]{:S(2)}, u32[]{:S(2)}) collective-permute-start(bf16[2,2,128,256]{3,2,1,0:T(8,128)(2,1)S(1)} %select_n.151), channel_id=1, source_target_pairs={{0,64},{64,0},{1,65},{65,1},{2,66},{66,2},{3,67},{67,3},{4,68},{68... | collective-permute-start | bytes 786440 | tf_op jit(solution)/shard_map/ppermute | solution.py:119
  39.7 13.6 %collective-permute-start.2 = (bf16[2,128,256]{2,1,0:T(8,128)(2,1)S(1)}, bf16[2,128,256]{2,1,0:T(8,128)(2,1)S(1)}, u32[]{:S(2)}, u32[]{:S(2)}) collective-permute-start(bf16[2,128,256]{2,1,0:T(8,128)(2,1)S(1)} %get-tuple-element.7), channel_id=1, source_target_pairs={{0,64},{64,0},{1,65},{65,1},{2,66},{66,2},{3,67},{67,3},{4,68},{68... | collective-permute-start | bytes 393224 | tf_op jit(solution)/shard_map/ppermute | solution.py:124
  42.8 22.2 %all-to-all-start.1 = ((bf16[32,8,512]{2,1,0:T(8,128)(2,1)}), bf16[32,8,512]{2,1,0:T(8,128)(2,1)S(1)}, u32[]{:S(2)}, u32[]{:S(2)}) async-start(bf16[32,8,512]{2,1,0:T(8,128)(2,1)} %bitcast.7), calls=%async_computation.1 | async-start | bytes 524288 | tf_op jit(solution)/shard_map/all_to_all | solution.py:131
  54.1 4.6 %collective-permute-start.3 = (bf16[128,512]{1,0:T(8,128)(2,1)S(1)}, bf16[128,512]{1,0:T(8,128)(2,1)S(1)}, u32[]{:S(2)}, u32[]{:S(2)}) collective-permute-start(bf16[128,512]{1,0:T(8,128)(2,1)S(1)} %squeeze.5), channel_id=1, source_target_pairs={{0,1},{1,0},{2,3},{3,2},{4,5},{5,4},{6,7},{7,6},{8,9},{9,8},{10,11... | collective-permute-start | bytes 393224 | tf_op jit(solution)/shard_map/ppermute | solution.py:128
  65.7 12.6 %all-to-all-start.2 = ((f32[8,4,256]{2,1,0:T(4,128)}), f32[8,4,256]{2,1,0:T(4,128)S(1)}, u32[]{:S(2)}, u32[]{:S(2)}) async-start(f32[8,4,256]{2,1,0:T(4,128)} %bitcast.12), calls=%async_computation.2 | async-start | bytes 65536 | tf_op jit(solution)/shard_map/all_to_all | solution.py:136

commit v2 on v0

v2 whole, which is shorter than its diff:
```python
import math

import jax
import jax.numpy as jnp
from jax import lax
from jax.experimental import pallas as pl
from jax.experimental.pallas import tpu as pltpu
from jax.sharding import Mesh, PartitionSpec as P

HD = 64
PAIR = 2 * HD
TAIL = 16
HELD = 4
WIDE = 8
SCALE = HD ** (-0.5)
LOG2E = 1.4426950408889634
BF16 = jnp.bfloat16
F32 = jnp.float32
HEAD_AXES = ("x", "ylo", "core")
SOURCE_AXES = ("z", "yhi")


def matmul(a, b):
    return lax.dot_general(a, b, (((1,), (0,)), ((), ())), preferred_element_type=F32)


def matmul_bt(a, b):
    return lax.dot_general(a, b, (((1,), (1,)), ((), ())), preferred_element_type=F32)


def split_lanes(a):
    first = lax.broadcasted_iota(jnp.int32, a.shape, 1) < HD
    zero = jnp.zeros_like(a)
    return jnp.concatenate([jnp.where(first, a, zero), jnp.where(first, zero, a)], axis=0)


def join(a, b, part):
    cols = slice(part * HD, (part + 1) * HD)
    return jnp.concatenate([a[:, cols], b[:, cols]], axis=1)


def pack_kernel(all_ref, out_ref):
    rows = out_ref.shape[1] - TAIL
    model = all_ref.shape[1]
    held = HELD
    zero = jnp.zeros((TAIL - held, PAIR), F32)
    for low in range(0, model, PAIR):
        cols = slice(low, low + PAIR)
        q, do = all_ref[:rows, cols], all_ref[rows : 2 * rows, cols]
        kv = all_ref[2 * rows :, cols].astype(F32)
        k, v = kv[:held], kv[held : 2 * held]
        for part in range(2):
            head = low // HD + part
            out_ref[head, :rows, :] = join(q, do, part)
            tail = jnp.concatenate([join(k, v, part), zero], axis=0)
            out_ref[head, rows:, :] = tail.astype(BF16)


def attention_kernel(x_ref, kv_ref, dq_ref, dkv_ref):
    sources = kv_ref.shape[0]
    blocks, rows = x_ref.shape[0], x_ref.shape[1] - TAIL
    kv = kv_ref[...]
    kv2 = split_lanes(kv)
    kt = kv.T[:HD]
    total = None
    for b in range(0, blocks, WIDE):
        x = jnp.concatenate([x_ref[b + i, :rows, :] for i in range(WIDE)], axis=0)
        both = matmul_bt(kv2, x)
        score = both[:sources] * (SCALE * LOG2E)
        dprob = both[sources:]
        expo = jnp.exp2(score - jnp.max(score, axis=0, keepdims=True))
        probs = expo * (1.0 / jnp.sum(expo, axis=0, keepdims=True))
        p_low = probs.astype(BF16)
        delta = jnp.sum(p_low.astype(F32) * dprob, axis=0, keepdims=True)
        ds_low = (probs * (dprob - delta)).astype(BF16)
        dq = (matmul(kt, ds_low) * SCALE).astype(BF16)
        for i in range(WIDE):
            dq_ref[b + i] = dq[:, i * rows : (i + 1) * rows]
        part = matmul(jnp.concatenate([ds_low, p_low], axis=1), split_lanes(x))
        total = part if total is None else total + part
    first = lax.broadcasted_iota(jnp.int32, total.shape, 1) < HD
    dkv_ref[...] = jnp.where(first, total * SCALE, total).astype(BF16)


def merge_kernel(dq_ref, parts_ref, out_ref):
    feats = dq_ref.shape[1]
    total = jnp.sum(parts_ref[...].astype(F32), axis=0)
    tail = jnp.concatenate([total, total], axis=0).astype(BF16)
    for b in range(dq_ref.shape[0]):
        out_ref[b, :feats, :] = dq_ref[b]
        out_ref[b, feats:, :] = tail


def finish_kernel(x_ref, dq_ref, dk_ref, dv_ref):
    heads = x_ref.shape[0]
    held = dk_ref.shape[0]
    for low in range(0, heads, 2):
        pair = jnp.concatenate([x_ref[low, :HD, :], x_ref[low + 1, :HD, :]], axis=0)
        dq_ref[:, low * HD : (low + 2) * HD] = pair.T
    group = lax.axis_index(("x", "ylo"))
    one = x_ref[2 * group, HD:, :].astype(F32)
    two = x_ref[2 * group + 1, HD:, :].astype(F32)
    lower = lax.axis_index("core") == 0
    one = jnp.where(lower, one[:held], one[held : 2 * held])
    two = jnp.where(lower, two[:held], two[held : 2 * held])
    dk_ref[...] = join(one, two, 0).astype(BF16)
    dv_ref[...] = join(one, two, 1).astype(BF16)


def call(kernel, out, *args, flops=0, transcendentals=0):
    vmem = pl.BlockSpec(memory_space=pltpu.VMEM)
    size = sum(a.size * a.dtype.itemsize for a in args) + sum(2 * math.prod(s) for s in out)
    return pl.pallas_call(
        kernel,
        out_shape=tuple(jax.ShapeDtypeStruct(s, BF16) for s in out),
        in_specs=[vmem] * len(args),
        out_specs=(vmem,) * len(out),
        compiler_params=pltpu.CompilerParams(vmem_limit_bytes=32 * 1024 * 1024),
        cost_estimate=pl.CostEstimate(flops=flops, bytes_accessed=size, transcendentals=transcendentals),
    )(*args)


def shards(queries, keys, values, out_grad):
    rows, model = queries.shape
    held = keys.shape[0]
    heads = model // HD
    chips = lax.axis_size(SOURCE_AXES)
    sources = 2 * held * chips

    none = jnp.zeros((TAIL - 2 * held, model), BF16)
    inputs = jnp.concatenate([queries, out_grad, keys, values, none], axis=0)
    (packed,) = call(pack_kernel, [(heads, rows + TAIL, PAIR)], inputs)
    packed = lax.all_to_all(packed, HEAD_AXES, 0, 0, tiled=True)
    block = jnp.concatenate([packed[0, rows : rows + held], packed[1, rows : rows + held]], axis=0)
    kv = lax.all_to_all(jnp.broadcast_to(block, (chips, 2 * held, PAIR)), SOURCE_AXES, 0, 0, tiled=True)

    pairs = heads * rows * sources
    dq, dkv = call(
        attention_kernel,
        [(heads, HD, rows), (sources, PAIR)],
        packed,
        kv.reshape(sources, PAIR),
        flops=16 * HD * pairs,
        transcendentals=pairs,
    )
    parts = lax.all_to_all(dkv.reshape(chips, 2 * held, PAIR), SOURCE_AXES, 0, 0, tiled=True)
    (merged,) = call(merge_kernel, [(heads, HD + TAIL, rows)], dq, parts)
    merged = lax.all_to_all(merged, HEAD_AXES, 0, 0, tiled=True)
    return call(finish_kernel, [(rows, model), (held, PAIR), (held, PAIR)], merged)


def solution(mesh):
    fine = Mesh(mesh.devices.reshape(4, 2, 8, 4, 2), ("x", "ylo", "z", "yhi", "core"))
    targets = ("x", "ylo", "z", "yhi", "core")
    sources = ("z", "yhi", "core")
    return jax.shard_map(
        shards,
        mesh=fine,
        in_specs=(P(targets, None), P(sources, None), P(sources, None), P(targets, None)),
        out_specs=(P(targets, None), P(sources, ("x", "ylo")), P(sources, ("x", "ylo"))),
        check_vma=False,
    )
```

time: 579 us -> 78 us (0.13)
  blocking collectives: 464 us -> 70.8 us
  local copies, waits for them, and re-layouts: 34.8 us -> 2.72 us
  waiting for transfers between devices: 31.8 us -> 0 us
  matrix products: 24.4 us -> 0 us
  between operations: 15.9 us -> 0.67 us
    unnamed x1 -> x0, blocking collectives: 295 us -> none
    all_gather x2 -> x0, blocking collectives: 170 us -> none  [the longest x1 91.8 us: shards(): lax.all_gather(values, 'blk', axis=0, tiled=True)]
    all_to_all x0 -> x4, blocking collectives: none -> 70.8 us  [the longest x1 23 us: shards(): lax.all_to_all(jnp.broadcast_to(block, (chips, 2 * held, PAIR)), SOURCE_A...]
    unnamed x2 -> x0, waiting for transfers between devices: 31.8 us -> none
    dot_general x40 -> x0, matrix products: 21 us -> none  [the longest x8 11.3 us: group_grads(): jnp.einsum('hrs,rhd->shd', dscore_low, q, preferred_element_type=jnp.floa...]
    reshape x24 -> x0, local copies, waits for them, and re-layouts: 19 us -> none  [the longest x8 11.5 us: group_grads(): dk.reshape(sources, 2 * HD)]
    unnamed x125 -> x4, local copies, waits for them, and re-layouts: 12.8 us -> 0.69 us
  transfers between devices with their start and end apart: 1 -> 0, of which waited for: 1 -> 0; matrix products, arithmetic and copies ran while one was open for 1% -> 0% of each run, Pallas kernels for 0% -> 0%
where the time goes in v2:
time: 78 us; the launch traced here: 77.6 us
  blocking collectives  70.8 us (91%)
  Pallas kernels  3.38 us (4%)
  local copies, waits for them, and re-layouts  2.72 us (3%)
    all_to_all x1, blocking collectives, shards(): lax.all_to_all(jnp.broadcast_to(block, (chips, 2 * held, PAIR)), SOURCE_A...  23 us
    all_to_all x1, blocking collectives, shards(): packed = lax.all_to_all(packed, HEAD_AXES, 0, 0, tiled=True)  20.6 us
    all_to_all x1, blocking collectives, shards(): lax.all_to_all(dkv.reshape(chips, 2 * held, PAIR), SOURCE_AXES, 0, 0, til...  14.1 us
    all_to_all x1, blocking collectives, shards(): merged = lax.all_to_all(merged, HEAD_AXES, 0, 0, tiled=True)  13.2 us
    pallas_call x4, Pallas kernels, call(): pl.pallas_call(kernel, out_shape=tuple((jax.ShapeDtypeStruct(s, BF16) for...  3.38 us
    concatenate x1, local copies, waits for them, and re-layouts, shards(): inputs = jnp.concatenate([queries, out_grad, keys, values, none], axis=0)  2.01 us

profile of v2, /device:TPU:1, one launch (start us, length us, event | category | flops | bytes accessed | tf_op | source)
XLA Modules:
  0.0 77.6 jit_solution(8868188757206081161)
XLA Ops:
  0.6 0.0 copy-start.1
  0.6 0.0 copy-start
  0.7 0.7 copy-done.1
  1.3 0.0 copy-done
  1.3 2.0 %concatenate.6.all_ref = bf16[272,1024]{1,0:T(8,128)(2,1)S(1)} concatenate(bf16[128,1024]{1,0:T(8,128)(2,1)} %param.4, bf16[128,1024]{1,0:T(8,128)(2,1)} %param.7, bf16[4,1024]{1,0:T(4,128)(2,1)S(1)} %copy-done, bf16[4,1024]{1,0:T(4,128)(2,1)S(1)} %copy-done.1, bf16[8,1024]{1,0:T(8,128)(2,1)S(1)} %broadcast_in_dim.6), dimensions={0} | concatenate | bytes 1114112 | tf_op jit(solution)/shard_map/concatenate | solution.py:131
  3.4 0.2 shard_map.67
  3.6 20.6 %all_to_all.20.x_ref = bf16[16,144,128]{2,1,0:T(8,128)(2,1)S(1)} all-to-all(bf16[16,144,128]{2,1,0:T(8,128)(2,1)S(1)} %shard_map.67), channel_id=1, replica_groups=mesh['x'=4,'ylo'=2,'z'=8,'yhi'=4,'core'=2] {'x','ylo','core'}, dimensions={0} | all-to-all | bytes 1179648 | tf_op jit(solution)/shard_map/all_to_all | solution.py:133
  24.2 23.0 %all_to_all.21 = bf16[32,8,128]{2,1,0:T(8,128)(2,1)S(1)} all-to-all(bf16[32,8,128]{2,1,0:T(8,128)(2,1)S(1)} %broadcast_in_dim.7), channel_id=1, replica_groups=mesh['x'=4,'ylo'=2,'z'=8,'yhi'=4,'core'=2] {'z','yhi'}, dimensions={0} | all-to-all | bytes 131072 | tf_op jit(solution)/shard_map/all_to_all | solution.py:135
  47.2 2.3 %shard_map.68 = (bf16[16,64,128]{2,1,0:T(8,128)(2,1)S(1)}, bf16[256,128]{1,0:T(8,128)(2,1)S(1)}) custom-call(bf16[16,144,128]{2,1,0:T(8,128)(2,1)S(1)} %all_to_all.20.x_ref, bf16[256,128]{1,0:T(8,128)(2,1)S(1)} %bitcast.6), custom_call_target="tpu_custom_call" | custom-call | flops 536870912 | bytes 983040 | tf_op jit(solution)/shard_map/pallas_call | solution.py:113
  49.5 14.1 %all_to_all.22.parts_ref = bf16[32,8,128]{2,1,0:T(8,128)(2,1)S(1)} all-to-all(bf16[32,8,128]{2,1,0:T(8,128)(2,1)S(1)} %bitcast.7), channel_id=1, replica_groups=mesh['x'=4,'ylo'=2,'z'=8,'yhi'=4,'core'=2] {'z','yhi'}, dimensions={0} | all-to-all | bytes 131072 | tf_op jit(solution)/shard_map/all_to_all | solution.py:146
  63.6 13.2 %all_to_all.23.x_ref = bf16[16,80,128]{2,1,0:T(8,128)(2,1)S(1)} all-to-all(bf16[16,80,128]{2,1,0:T(8,128)(2,1)S(1)} %shard_map.69), channel_id=1, replica_groups=mesh['x'=4,'ylo'=2,'z'=8,'yhi'=4,'core'=2] {'x','ylo','core'}, dimensions={0} | all-to-all | bytes 655360 | tf_op jit(solution)/shard_map/all_to_all | solution.py:148
  76.8 0.8 %shard_map.70 = (bf16[128,1024]{1,0:T(8,128)(2,1)}, bf16[4,128]{1,0:T(4,128)(2,1)}, bf16[4,128]{1,0:T(4,128)(2,1)}) custom-call(bf16[16,80,128]{2,1,0:T(8,128)(2,1)S(1)} %all_to_all.23.x_ref), custom_call_target="tpu_custom_call" | custom-call | bytes 591872 | tf_op jit(solution)/shard_map/pallas_call | solution.py:113
  (5 shorter events, 0.1 us)
Async XLA Ops:
  0.6 0.7 copy-start.1
  0.6 0.7 copy-start

commit v3 on v2

v3 whole, which is shorter than its diff:
```python
import math

import jax
import jax.numpy as jnp
from jax import lax
from jax.experimental import pallas as pl
from jax.experimental.pallas import tpu as pltpu
from jax.sharding import Mesh, PartitionSpec as P

HD = 64
PAIR = 2 * HD
SCALE = HD ** (-0.5)
LOG2E = 1.4426950408889634
BF16 = jnp.bfloat16
F32 = jnp.float32
SOURCE_AXES = ("z", "yhi")
CORE_SWAP = [(0, 1), (1, 0)]
BOTH_SWAP = [(0, 3), (1, 2), (2, 1), (3, 0)]


def matmul(a, b):
    return lax.dot_general(a, b, (((1,), (0,)), ((), ())), preferred_element_type=F32)


def matmul_bt(a, b):
    return lax.dot_general(a, b, (((1,), (1,)), ((), ())), preferred_element_type=F32)


def split_lanes(a):
    first = lax.broadcasted_iota(jnp.int32, a.shape, 1) < HD
    zero = jnp.zeros_like(a)
    return jnp.concatenate([jnp.where(first, a, zero), jnp.where(first, zero, a)], axis=0)


def columns(core, side, pair):
    return pl.ds(pl.multiple_of((4 * core + 2 * pair + side) * PAIR, PAIR), PAIR)


def spread_kernel(k_ref, v_ref, out_ref):
    side = lax.axis_index("ylo")
    for core in range(2):
        parts = [ref[:, columns(core, side, pair)] for ref in (k_ref, v_ref) for pair in range(2)]
        block = jnp.concatenate(parts, axis=1)
        for chip in range(out_ref.shape[0] // 2):
            out_ref[2 * chip + core] = block


def quarter_kernel(q_ref, do_ref, *out_refs):
    core, side = lax.axis_index("core"), lax.axis_index("ylo")
    for at, out_ref in enumerate(out_refs):
        for pair in range(2):
            cols = columns(core ^ (at & 1), side ^ (at >> 1), pair)
            low = slice(pair * PAIR, (pair + 1) * PAIR)
            out_ref[0, :, low] = q_ref[:, cols]
            out_ref[1, :, low] = do_ref[:, cols]


def attention_kernel(*refs):
    in_refs, kv_ref, dq_refs, dkv_ref, flat_ref = refs[:4], refs[4], refs[5:9], refs[9], refs[10]
    held = kv_ref.shape[1]
    for at in range(kv_ref.shape[0]):
        flat_ref[at * held : (at + 1) * held, :] = kv_ref[at].astype(F32)
    sources, width = flat_ref.shape[0], flat_ref.shape[1] // 2
    rows = in_refs[0].shape[1]
    for low in range(0, width, PAIR):
        cols = slice(low, low + PAIR)
        k2 = split_lanes(flat_ref[:, cols].astype(BF16))
        v2 = split_lanes(flat_ref[:, width + low : width + low + PAIR].astype(BF16))
        q = jnp.concatenate([ref[0, :, cols] for ref in in_refs], axis=0)
        do = jnp.concatenate([ref[1, :, cols] for ref in in_refs], axis=0)
        score = (matmul_bt(k2, q) * (SCALE * LOG2E)).reshape(2, sources, 4 * rows)
        dprob = matmul_bt(v2, do).reshape(2, sources, 4 * rows)
        expo = jnp.exp2(score - jnp.max(score, axis=1, keepdims=True))
        probs = expo * (1.0 / jnp.sum(expo, axis=1, keepdims=True))
        p_low = probs.astype(BF16)
        delta = jnp.sum(p_low.astype(F32) * dprob, axis=1, keepdims=True)
        ds_low = (probs * (dprob - delta)).astype(BF16)
        dk = matmul(jnp.concatenate([ds_low[0], ds_low[1]], axis=1), split_lanes(q)) * SCALE
        dv = matmul(jnp.concatenate([p_low[0], p_low[1]], axis=1), split_lanes(do))
        dkv_ref[:, cols] = dk.astype(BF16)
        dkv_ref[:, width + low : width + low + PAIR] = dv.astype(BF16)
        dq_t = (matmul(k2.T, ds_low.reshape(2 * sources, 4 * rows)) * SCALE).astype(BF16)
        for at, dq_ref in enumerate(dq_refs):
            dq_ref[:, cols] = dq_t[:, at * rows : (at + 1) * rows].T


def reduce_kernel(parts_ref, out_ref):
    total = jnp.sum(parts_ref[...].astype(F32), axis=0)
    held, width = out_ref.shape[1], total.shape[1] // 2
    core = lax.axis_index("core")
    for dest in range(out_ref.shape[0]):
        x, half = dest // 2, dest % 2
        low = (x % 2) * PAIR
        rows = total[half * held : (half + 1) * held]
        piece = jnp.concatenate([rows[:, low : low + PAIR], rows[:, width + low : width + low + PAIR]], axis=1)
        out_ref[dest] = jnp.where(core == x // 2, piece, jnp.zeros_like(piece))


def finish_kernel(own_ref, core_ref, side_ref, both_ref, mine_ref, dq_ref, dk_ref, dv_ref):
    core, side = lax.axis_index("core"), lax.axis_index("ylo")
    for at, ref in enumerate((own_ref, core_ref, side_ref, both_ref)):
        for pair in range(2):
            dq_ref[:, columns(core ^ (at & 1), side ^ (at >> 1), pair)] = ref[:, pair * PAIR : (pair + 1) * PAIR]
    total = jnp.sum(mine_ref[...], axis=0)
    dk_ref[...] = total[:, :PAIR].astype(BF16)
    dv_ref[...] = total[:, PAIR:].astype(BF16)


def call(kernel, out, *args, dtype=BF16, scratch=(), flops=0, transcendentals=0):
    vmem = pl.BlockSpec(memory_space=pltpu.VMEM)
    size = sum(a.size * a.dtype.itemsize for a in args) + sum(2 * math.prod(s) for s in out)
    return pl.pallas_call(
        kernel,
        out_shape=tuple(jax.ShapeDtypeStruct(s, dtype) for s in out),
        in_specs=[vmem] * len(args),
        out_specs=(vmem,) * len(out),
        scratch_shapes=scratch,
        compiler_params=pltpu.CompilerParams(vmem_limit_bytes=32 * 1024 * 1024),
        cost_estimate=pl.CostEstimate(flops=flops, bytes_accessed=size, transcendentals=transcendentals),
    )(*args)


def trade(arrays):
    own, core, side, both = arrays
    core = lax.ppermute(core, "core", CORE_SWAP)
    side = lax.ppermute(side, "ylo", CORE_SWAP)
    both = lax.ppermute(both, ("ylo", "core"), BOTH_SWAP)
    return own, core, side, both


def shards(queries, keys, values, out_grad):
    rows, model = queries.shape
    held = keys.shape[0]
    width = model // 4
    chips = lax.axis_size(SOURCE_AXES)
    sources = 2 * held * chips

    (spread,) = call(spread_kernel, [(2 * chips, held, 2 * width)], keys, values)
    kv = lax.all_to_all(spread, SOURCE_AXES + ("core",), 0, 0, tiled=True)
    targets = trade(call(quarter_kernel, [(2, rows, width)] * 4, queries, out_grad))

    pairs = 4 * rows * sources * width // HD
    *dq, dkv = call(
        attention_kernel,
        [(rows, width)] * 4 + [(sources, 2 * width)],
        *targets,
        kv,
        scratch=[pltpu.VMEM((sources, 2 * width), F32)],
        flops=20 * HD * pairs,
        transcendentals=pairs,
    )
    parts = lax.all_to_all(dkv.reshape(chips, 2 * held, 2 * width), SOURCE_AXES, 0, 0, tiled=True)
    dq = trade(dq)
    (outgoing,) = call(reduce_kernel, [(8, held, 2 * PAIR)], parts, dtype=F32)
    mine = lax.all_to_all(outgoing, ("x", "core"), 0, 0, tiled=True)
    return call(finish_kernel, [(rows, model), (held, PAIR), (held, PAIR)], *dq, mine)


def solution(mesh):
    fine = Mesh(mesh.devices.reshape(4, 2, 8, 4, 2), ("x", "ylo", "z", "yhi", "core"))
    targets = ("x", "ylo", "z", "yhi", "core")
    sources = ("z", "yhi", "core")
    return jax.shard_map(
        shards,
        mesh=fine,
        in_specs=(P(targets, None), P(sources, None), P(sources, None), P(targets, None)),
        out_specs=(P(targets, None), P(sources, ("x", "ylo")), P(sources, ("x", "ylo"))),
        check_vma=False,
    )
```

time: 78 us -> 73.9 us (0.947)
  blocking collectives: 70.8 us -> 0 us
  starting transfers between devices: 0 us -> 50.2 us
  waiting for transfers between devices: 0 us -> 15.7 us
  Pallas kernels: 3.38 us -> 5.21 us
  local copies, waits for them, and re-layouts: 2.72 us -> 1.39 us
    all_to_all x4 -> x0, blocking collectives: 70.8 us -> none  [the longest x1 23 us: shards(): lax.all_to_all(jnp.broadcast_to(block, (chips, 2 * held, PAIR)), SOURCE_A...]
    all_to_all x0 -> x3, starting transfers between devices: none -> 34.3 us  [the longest x1 17.8 us: shards(): kv = lax.all_to_all(spread, SOURCE_AXES + ('core',), 0, 0, tiled=True)]
    ppermute x0 -> x6, starting transfers between devices: none -> 15.9 us  [the longest x2 5.99 us: trade(): both = lax.ppermute(both, ('ylo', 'core'), BOTH_SWAP)]
    all_to_all x0 -> x3, waiting for transfers between devices: none -> 10.4 us  [the longest x1 4.7 us: shards(): mine = lax.all_to_all(outgoing, ('x', 'core'), 0, 0, tiled=True)]
    ppermute x0 -> x6, waiting for transfers between devices: none -> 5.32 us  [the longest x2 3.01 us: trade(): both = lax.ppermute(both, ('ylo', 'core'), BOTH_SWAP)]
    concatenate x1 -> x0, local copies, waits for them, and re-layouts: 2.01 us -> none  [shards(): inputs = jnp.concatenate([queries, out_grad, keys, values, none], axis=0)]
    pallas_call x4 -> x5, Pallas kernels: 3.38 us -> 5.21 us  [call(): pl.pallas_call(kernel, out_shape=tuple((jax.ShapeDtypeStruct(s, dtype) fo...]
  transfers between devices with their start and end apart: 0 -> 9, of which waited for: 0 -> 5; matrix products, arithmetic and copies ran while one was open for 0% -> 0% of each run, Pallas kernels for 0% -> 1%
where the time goes in v3:
time: 73.9 us; the launch traced here: 73.3 us
  starting transfers between devices  50.2 us (68%)
  waiting for transfers between devices  15.7 us (21%)
  Pallas kernels  5.21 us (7%)
  local copies, waits for them, and re-layouts  1.39 us (2%)
  between operations  0.75 us (1%)
    all_to_all x1, starting transfers between devices, shards(): kv = lax.all_to_all(spread, SOURCE_AXES + ('core',), 0, 0, tiled=True)  17.8 us
    all_to_all x1, starting transfers between devices, shards(): lax.all_to_all(dkv.reshape(chips, 2 * held, 2 * width), SOURCE_AXES, 0, 0...  9.22 us
    all_to_all x1, starting transfers between devices, shards(): mine = lax.all_to_all(outgoing, ('x', 'core'), 0, 0, tiled=True)  7.3 us
    ppermute x2, starting transfers between devices, trade(): both = lax.ppermute(both, ('ylo', 'core'), BOTH_SWAP)  5.99 us
    pallas_call x5, Pallas kernels, call(): pl.pallas_call(kernel, out_shape=tuple((jax.ShapeDtypeStruct(s, dtype) fo...  5.21 us
    ppermute x2, starting transfers between devices, trade(): side = lax.ppermute(side, 'ylo', CORE_SWAP)  4.97 us
    ppermute x2, starting transfers between devices, trade(): core = lax.ppermute(core, 'core', CORE_SWAP)  4.95 us
    all_to_all x1, waiting for transfers between devices, shards(): mine = lax.all_to_all(outgoing, ('x', 'core'), 0, 0, tiled=True)  4.7 us
  transfers between devices with their start and end apart: 9, of which 5 were waited for; matrix products, arithmetic and copies ran while one was open for 0% of the time, Pallas kernels for 1%

profile of v3, /device:TPU:1, one launch (start us, length us, event | category | flops | bytes accessed | tf_op | source)
XLA Modules:
  0.0 73.3 jit_solution(11966456056773784264)
XLA Ops:
  0.6 0.0 copy-start.2
  0.6 0.7 copy-done.2
  1.3 0.0 copy-start.3
  1.3 0.7 copy-done.3
  2.0 0.7 shard_map.68
  2.8 0.0 copy-start
  2.8 0.0 copy-start.1
  2.8 17.8 %all-to-all-start = ((bf16[64,4,512]{2,1,0:T(4,128)(2,1)}), bf16[64,4,512]{2,1,0:T(4,128)(2,1)S(1)}, u32[]{:S(2)}, u32[]{:S(2)}) async-start(bf16[64,4,512]{2,1,0:T(4,128)(2,1)} %shard_map.68), calls=%async_computation | async-start | bytes 524288 | tf_op jit(solution)/shard_map/all_to_all | solution.py:139
  20.5 0.0 copy-done
  20.5 0.0 copy-done.1
  20.6 0.1 shard_map.67
  20.7 2.4 %collective-permute-start = (bf16[2,128,256]{2,1,0:T(8,128)(2,1)S(1)}, bf16[2,128,256]{2,1,0:T(8,128)(2,1)S(1)}, u32[]{:S(2)}, u32[]{:S(2)}) collective-permute-start(bf16[2,128,256]{2,1,0:T(8,128)(2,1)S(1)} %get-tuple-element.13), channel_id=1, source_target_pairs={{0,1},{1,0},{2,3},{3,2},{4,5},{5,4},{6,7},{7,6},{8,9},{9,8},{10,11... | collective-permute-start | bytes 393224 | tf_op jit(solution)/shard_map/ppermute | solution.py:125
  23.1 2.3 %collective-permute-start.1 = (bf16[2,128,256]{2,1,0:T(8,128)(2,1)S(1)}, bf16[2,128,256]{2,1,0:T(8,128)(2,1)S(1)}, u32[]{:S(2)}, u32[]{:S(2)}) collective-permute-start(bf16[2,128,256]{2,1,0:T(8,128)(2,1)S(1)} %get-tuple-element.14), channel_id=1, source_target_pairs={{0,64},{64,0},{1,65},{65,1},{2,66},{66,2},{3,67},{67,3},{4,68},{68... | collective-permute-start | bytes 393224 | tf_op jit(solution)/shard_map/ppermute | solution.py:126
  25.4 3.2 %collective-permute-start.2 = (bf16[2,128,256]{2,1,0:T(8,128)(2,1)S(1)}, bf16[2,128,256]{2,1,0:T(8,128)(2,1)S(1)}, u32[]{:S(2)}, u32[]{:S(2)}) collective-permute-start(bf16[2,128,256]{2,1,0:T(8,128)(2,1)S(1)} %get-tuple-element.15), channel_id=1, source_target_pairs={{0,65},{1,64},{64,1},{65,0},{2,67},{3,66},{66,3},{67,2},{4,69},{5,... | collective-permute-start | bytes 393224 | tf_op jit(solution)/shard_map/ppermute | solution.py:127
  28.6 0.0 collective-permute-done.refs_1_
  28.6 2.3 %collective-permute-done.1.refs_2_ = bf16[2,128,256]{2,1,0:T(8,128)(2,1)S(1)} collective-permute-done((bf16[2,128,256]{2,1,0:T(8,128)(2,1)S(1)}, bf16[2,128,256]{2,1,0:T(8,128)(2,1)S(1)}, u32[]{:S(2)}, u32[]{:S(2)}) %collective-permute-start.1) | collective-permute-done | bytes 131104 | tf_op jit(solution)/shard_map/ppermute | solution.py:126
  30.9 3.0 %collective-permute-done.2.refs_3_ = bf16[2,128,256]{2,1,0:T(8,128)(2,1)S(1)} collective-permute-done((bf16[2,128,256]{2,1,0:T(8,128)(2,1)S(1)}, bf16[2,128,256]{2,1,0:T(8,128)(2,1)S(1)}, u32[]{:S(2)}, u32[]{:S(2)}) %collective-permute-start.2) | collective-permute-done | bytes 131104 | tf_op jit(solution)/shard_map/ppermute | solution.py:127
  33.9 1.9 %all-to-all-done.refs_4_ = bf16[64,4,512]{2,1,0:T(4,128)(2,1)S(1)} async-done(((bf16[64,4,512]{2,1,0:T(4,128)(2,1)}), bf16[64,4,512]{2,1,0:T(4,128)(2,1)S(1)}, u32[]{:S(2)}, u32[]{:S(2)}) %all-to-all-start) | async-done | bytes 262176 | tf_op jit(solution)/shard_map/all_to_all | solution.py:139
  35.8 2.9 %shard_map.69 = (bf16[128,256]{1,0:T(8,128)(2,1)S(1)}, bf16[128,256]{1,0:T(8,128)(2,1)S(1)}, bf16[128,256]{1,0:T(8,128)(2,1)S(1)}, bf16[128,256]{1,0:T(8,128)(2,1)S(1)}, bf16[256,512]{1,0:T(8,128)(2,1)}) custom-call(bf16[2,128,256]{2,1,0:T(8,128)(2,1)S(1)} %get-tuple-element.12.refs_0_, bf16[2,128,256]{2,1,0:T(8,128)(2,1)S(1)} %collective-permute-done.refs_1_, ...), custom_call_target="tpu_custom_call" | custom-call | flops 671088640 | bytes 1310720 | tf_op jit(solution)/shard_map/pallas_call | solution.py:112
  38.7 9.2 %all-to-all-start.1 = ((bf16[32,8,512]{2,1,0:T(8,128)(2,1)}), bf16[32,8,512]{2,1,0:T(8,128)(2,1)S(1)}, u32[]{:S(2)}, u32[]{:S(2)}) async-start(bf16[32,8,512]{2,1,0:T(8,128)(2,1)} %bitcast), calls=%async_computation.1 | async-start | bytes 524288 | tf_op jit(solution)/shard_map/all_to_all | solution.py:152
  47.9 2.6 %collective-permute-start.3 = (bf16[128,256]{1,0:T(8,128)(2,1)S(1)}, bf16[128,256]{1,0:T(8,128)(2,1)S(1)}, u32[]{:S(2)}, u32[]{:S(2)}) collective-permute-start(bf16[128,256]{1,0:T(8,128)(2,1)S(1)} %get-tuple-element.17), channel_id=1, source_target_pairs={{0,1},{1,0},{2,3},{3,2},{4,5},{5,4},{6,7},{7,6},{8,9},{9,8},{10,11... | collective-permute-start | bytes 196616 | tf_op jit(solution)/shard_map/ppermute | solution.py:125
  50.5 2.7 %collective-permute-start.4 = (bf16[128,256]{1,0:T(8,128)(2,1)S(1)}, bf16[128,256]{1,0:T(8,128)(2,1)S(1)}, u32[]{:S(2)}, u32[]{:S(2)}) collective-permute-start(bf16[128,256]{1,0:T(8,128)(2,1)S(1)} %get-tuple-element.18), channel_id=1, source_target_pairs={{0,64},{64,0},{1,65},{65,1},{2,66},{66,2},{3,67},{67,3},{4,68},{68... | collective-permute-start | bytes 196616 | tf_op jit(solution)/shard_map/ppermute | solution.py:126
  53.2 2.8 %collective-permute-start.5 = (bf16[128,256]{1,0:T(8,128)(2,1)S(1)}, bf16[128,256]{1,0:T(8,128)(2,1)S(1)}, u32[]{:S(2)}, u32[]{:S(2)}) collective-permute-start(bf16[128,256]{1,0:T(8,128)(2,1)S(1)} %get-tuple-element.19), channel_id=1, source_target_pairs={{0,65},{1,64},{64,1},{65,0},{2,67},{3,66},{66,3},{67,2},{4,69},{5,... | collective-permute-start | bytes 196616 | tf_op jit(solution)/shard_map/ppermute | solution.py:127
  56.0 3.8 %all-to-all-done.1.parts_ref = bf16[32,8,512]{2,1,0:T(8,128)(2,1)S(1)} async-done(((bf16[32,8,512]{2,1,0:T(8,128)(2,1)}), bf16[32,8,512]{2,1,0:T(8,128)(2,1)S(1)}, u32[]{:S(2)}, u32[]{:S(2)}) %all-to-all-start.1) | async-done | bytes 262176 | tf_op jit(solution)/shard_map/all_to_all | solution.py:152
  59.8 0.7 shard_map.70
  60.5 7.3 %all-to-all-start.2 = ((f32[8,4,256]{2,1,0:T(4,128)}), f32[8,4,256]{2,1,0:T(4,128)S(1)}, u32[]{:S(2)}, u32[]{:S(2)}) async-start(f32[8,4,256]{2,1,0:T(4,128)} %shard_map.70), calls=%async_computation.2 | async-start | bytes 65536 | tf_op jit(solution)/shard_map/all_to_all | solution.py:155
  67.8 0.0 collective-permute-done.3.core_ref
  67.8 0.0 collective-permute-done.4.side_ref
  67.8 0.0 collective-permute-done.5.both_ref
  67.8 4.7 %all-to-all-done.2.mine_ref = f32[8,4,256]{2,1,0:T(4,128)S(1)} async-done(((f32[8,4,256]{2,1,0:T(4,128)}), f32[8,4,256]{2,1,0:T(4,128)S(1)}, u32[]{:S(2)}, u32[]{:S(2)}) %all-to-all-start.2) | async-done | bytes 32800 | tf_op jit(solution)/shard_map/all_to_all | solution.py:155
  72.5 0.8 %shard_map.71 = (bf16[128,1024]{1,0:T(8,128)(2,1)}, bf16[4,128]{1,0:T(4,128)(2,1)}, bf16[4,128]{1,0:T(4,128)(2,1)}) custom-call(bf16[128,256]{1,0:T(8,128)(2,1)S(1)} %get-tuple-element.16.own_ref, bf16[128,256]{1,0:T(8,128)(2,1)S(1)} %collective-permute-done.3.core_ref, bf16[128,256]{1,0:T(8,128)(2,1)S(1)} %collective-permute-done.4.side_ref, ...), custom_call_target="tpu_custom_call" | custom-call | bytes 559104 | tf_op jit(solution)/shard_map/pallas_call | solution.py:112
Async XLA Ops:
  0.6 0.7 copy-start.2
  1.3 0.7 copy-start.3
  2.8 17.8 %copy-start = (bf16[128,1024]{1,0:T(8,128)(2,1)S(1)}, bf16[128,1024]{1,0:T(8,128)(2,1)}, u32[]{:S(2)}) copy-start(bf16[128,1024]{1,0:T(8,128)(2,1)} %q_ref.1) | copy-start | bytes 786436
  2.8 17.8 %copy-start.1 = (bf16[128,1024]{1,0:T(8,128)(2,1)S(1)}, bf16[128,1024]{1,0:T(8,128)(2,1)}, u32[]{:S(2)}) copy-start(bf16[128,1024]{1,0:T(8,128)(2,1)} %do_ref.1) | copy-start | bytes 786436
  2.8 33.0 %all-to-all-start = ((bf16[64,4,512]{2,1,0:T(4,128)(2,1)}), bf16[64,4,512]{2,1,0:T(4,128)(2,1)S(1)}, u32[]{:S(2)}, u32[]{:S(2)}) async-start(bf16[64,4,512]{2,1,0:T(4,128)(2,1)} %shard_map.68), calls=%async_computation | async-start | bytes 524288 | tf_op jit(solution)/shard_map/all_to_all | solution.py:139
  20.7 7.9 %collective-permute-start = (bf16[2,128,256]{2,1,0:T(8,128)(2,1)S(1)}, bf16[2,128,256]{2,1,0:T(8,128)(2,1)S(1)}, u32[]{:S(2)}, u32[]{:S(2)}) collective-permute-start(bf16[2,128,256]{2,1,0:T(8,128)(2,1)S(1)} %get-tuple-element.13), channel_id=1, source_target_pairs={{0,1},{1,0},{2,3},{3,2},{4,5},{5,4},{6,7},{7,6},{8,9},{9,8},{10,11... | collective-permute-start | bytes 393224 | tf_op jit(solution)/shard_map/ppermute | solution.py:125
  23.1 7.8 %collective-permute-start.1 = (bf16[2,128,256]{2,1,0:T(8,128)(2,1)S(1)}, bf16[2,128,256]{2,1,0:T(8,128)(2,1)S(1)}, u32[]{:S(2)}, u32[]{:S(2)}) collective-permute-start(bf16[2,128,256]{2,1,0:T(8,128)(2,1)S(1)} %get-tuple-element.14), channel_id=1, source_target_pairs={{0,64},{64,0},{1,65},{65,1},{2,66},{66,2},{3,67},{67,3},{4,68},{68... | collective-permute-start | bytes 393224 | tf_op jit(solution)/shard_map/ppermute | solution.py:126
  25.4 8.5 %collective-permute-start.2 = (bf16[2,128,256]{2,1,0:T(8,128)(2,1)S(1)}, bf16[2,128,256]{2,1,0:T(8,128)(2,1)S(1)}, u32[]{:S(2)}, u32[]{:S(2)}) collective-permute-start(bf16[2,128,256]{2,1,0:T(8,128)(2,1)S(1)} %get-tuple-element.15), channel_id=1, source_target_pairs={{0,65},{1,64},{64,1},{65,0},{2,67},{3,66},{66,3},{67,2},{4,69},{5,... | collective-permute-start | bytes 393224 | tf_op jit(solution)/shard_map/ppermute | solution.py:127
  38.7 21.1 %all-to-all-start.1 = ((bf16[32,8,512]{2,1,0:T(8,128)(2,1)}), bf16[32,8,512]{2,1,0:T(8,128)(2,1)S(1)}, u32[]{:S(2)}, u32[]{:S(2)}) async-start(bf16[32,8,512]{2,1,0:T(8,128)(2,1)} %bitcast), calls=%async_computation.1 | async-start | bytes 524288 | tf_op jit(solution)/shard_map/all_to_all | solution.py:152
  47.9 19.9 %collective-permute-start.3 = (bf16[128,256]{1,0:T(8,128)(2,1)S(1)}, bf16[128,256]{1,0:T(8,128)(2,1)S(1)}, u32[]{:S(2)}, u32[]{:S(2)}) collective-permute-start(bf16[128,256]{1,0:T(8,128)(2,1)S(1)} %get-tuple-element.17), channel_id=1, source_target_pairs={{0,1},{1,0},{2,3},{3,2},{4,5},{5,4},{6,7},{7,6},{8,9},{9,8},{10,11... | collective-permute-start | bytes 196616 | tf_op jit(solution)/shard_map/ppermute | solution.py:125
  50.5 17.3 %collective-permute-start.4 = (bf16[128,256]{1,0:T(8,128)(2,1)S(1)}, bf16[128,256]{1,0:T(8,128)(2,1)S(1)}, u32[]{:S(2)}, u32[]{:S(2)}) collective-permute-start(bf16[128,256]{1,0:T(8,128)(2,1)S(1)} %get-tuple-element.18), channel_id=1, source_target_pairs={{0,64},{64,0},{1,65},{65,1},{2,66},{66,2},{3,67},{67,3},{4,68},{68... | collective-permute-start | bytes 196616 | tf_op jit(solution)/shard_map/ppermute | solution.py:126
  53.2 14.6 %collective-permute-start.5 = (bf16[128,256]{1,0:T(8,128)(2,1)S(1)}, bf16[128,256]{1,0:T(8,128)(2,1)S(1)}, u32[]{:S(2)}, u32[]{:S(2)}) collective-permute-start(bf16[128,256]{1,0:T(8,128)(2,1)S(1)} %get-tuple-element.19), channel_id=1, source_target_pairs={{0,65},{1,64},{64,1},{65,0},{2,67},{3,66},{66,3},{67,2},{4,69},{5,... | collective-permute-start | bytes 196616 | tf_op jit(solution)/shard_map/ppermute | solution.py:127
  60.5 12.0 %all-to-all-start.2 = ((f32[8,4,256]{2,1,0:T(4,128)}), f32[8,4,256]{2,1,0:T(4,128)S(1)}, u32[]{:S(2)}, u32[]{:S(2)}) async-start(f32[8,4,256]{2,1,0:T(4,128)} %shard_map.70), calls=%async_computation.2 | async-start | bytes 65536 | tf_op jit(solution)/shard_map/all_to_all | solution.py:155

commit v4 on v3

v4 whole, which is shorter than its diff:
```python
import functools
import itertools
import math

import jax
import jax.numpy as jnp
from jax import lax
from jax.experimental import pallas as pl
from jax.experimental.pallas import tpu as pltpu
from jax.sharding import Mesh, PartitionSpec as P

HD = 64
PAIR = 2 * HD
SCALE = HD ** (-0.5)
LOG2E = 1.4426950408889634
BF16 = jnp.bfloat16
F32 = jnp.float32
AXES = ("xh", "xl", "ylo", "z", "yhi", "core")
SOURCE_AXES = ("z", "yhi", "core")
GRAD_AXES = ("xh", "ylo", "z", "yhi", "core")
SOURCE_FIRST = (7, 2, 0)
GRAD_FIRST = (0, 0, 4, 0, 0)
CORE_SWAP = [(0, 1), (1, 0)]
BOTH_SWAP = [(0, 3), (1, 2), (2, 1), (3, 0)]


def matmul(a, b):
    return lax.dot_general(a, b, (((1,), (0,)), ((), ())), preferred_element_type=F32)


def matmul_bt(a, b):
    return lax.dot_general(a, b, (((1,), (1,)), ((), ())), preferred_element_type=F32)


def split_lanes(a):
    first = lax.broadcasted_iota(jnp.int32, a.shape, 1) < HD
    zero = jnp.zeros_like(a)
    return jnp.concatenate([jnp.where(first, a, zero), jnp.where(first, zero, a)], axis=0)


def join(a, b, part):
    cols = slice(part * HD, (part + 1) * HD)
    return jnp.concatenate([a[:, cols], b[:, cols]], axis=1)


def columns(side, pair, x):
    return pl.ds(pl.multiple_of((4 * pair + 2 * side + x) * PAIR, PAIR), PAIR)


def core_columns(ref, side, pair):
    a, b = (ref[:, columns(side, pair, x)].astype(F32) for x in range(2))
    return join(a, b, 0).astype(ref.dtype), join(a, b, 1).astype(ref.dtype)


def spread_kernel(kv_ref, out_ref):
    side = lax.axis_index("xl")
    held = out_ref.shape[1]
    pieces = []
    for pair in range(2):
        a, b = (kv_ref[:, columns(side, pair, x)].astype(F32) for x in range(2))
        pieces.append([join(a, b, core) for core in range(2)])
    for core in range(2):
        parts = [piece[core][low : low + held] for low in (0, held) for piece in pieces]
        block = jnp.concatenate(parts, axis=1).astype(BF16)
        for chip in range(out_ref.shape[0] // 2):
            out_ref[2 * chip + core] = block


def quarter_kernel(q_ref, do_ref, *out_refs):
    lower, side = lax.axis_index("core") == 0, lax.axis_index("xl")
    for flip in range(2):
        for pair in range(2):
            low = slice(pair * PAIR, (pair + 1) * PAIR)
            for at, ref in enumerate((q_ref, do_ref)):
                one, two = core_columns(ref, side ^ flip, pair)
                out_refs[flip][at, :, low] = jnp.where(lower, one, two)
                out_refs[3 - flip][at, :, low] = jnp.where(lower, two, one)


def attention_kernel(source_order, grad_order, *refs):
    in_refs, kv_ref, dq_refs, dkv_hbm, flat_ref, dkv_ref, sems = refs[:4], refs[4], refs[5:9], *refs[9:]
    held = kv_ref.shape[1]
    for at, block in enumerate(source_order):
        flat_ref[block * held : (block + 1) * held, :] = kv_ref[at].astype(F32)
    sources, width = flat_ref.shape[0], flat_ref.shape[1] // 2
    blocks = sources // held
    places = {member: at for at, member in enumerate(grad_order)}
    rows = in_refs[0].shape[1]
    copies = []
    for low in range(0, width, PAIR):
        cols = slice(low, low + PAIR)
        k2 = split_lanes(flat_ref[:, cols].astype(BF16))
        v2 = split_lanes(flat_ref[:, width + low : width + low + PAIR].astype(BF16))
        q = jnp.concatenate([ref[0, :, cols] for ref in in_refs], axis=0)
        do = jnp.concatenate([ref[1, :, cols] for ref in in_refs], axis=0)
        score = (matmul_bt(k2, q) * (SCALE * LOG2E)).reshape(2, sources, 4 * rows)
        dprob = matmul_bt(v2, do).reshape(2, sources, 4 * rows)
        expo = jnp.exp2(score - jnp.max(score, axis=1, keepdims=True))
        probs = expo * (1.0 / jnp.sum(expo, axis=1, keepdims=True))
        p_low = probs.astype(BF16)
        delta = jnp.sum(p_low.astype(F32) * dprob, axis=1, keepdims=True)
        ds_low = (probs * (dprob - delta)).astype(BF16)
        dk = matmul(jnp.concatenate([ds_low[0], ds_low[1]], axis=1), split_lanes(q)) * SCALE
        dv = matmul(jnp.concatenate([p_low[0], p_low[1]], axis=1), split_lanes(do))
        for part in range(2):
            both = join(dk, dv, part)
            first = (low // HD + part) * blocks
            for at in range(blocks):
                dkv_ref[places[first + at]] = both[at * held : (at + 1) * held].astype(BF16)
            span = pl.ds(places[first] // blocks * blocks, blocks)
            copy = pltpu.make_async_copy(dkv_ref.at[span], dkv_hbm.at[span], sems.at[low // HD + part])
            copy.start()
            copies.append(copy)
        dq_t = (matmul(k2.T, ds_low.reshape(2 * sources, 4 * rows)) * SCALE).astype(BF16)
        for at, dq_ref in enumerate(dq_refs):
            dq_ref[:, cols] = dq_t[:, at * rows : (at + 1) * rows].T
    for copy in copies:
        copy.wait()


def assemble_kernel(own_ref, side_ref, both_ref, core_ref, dq_ref):
    lower, side = lax.axis_index("core") == 0, lax.axis_index("xl")
    for flip, (near_ref, far_ref) in enumerate(((own_ref, core_ref), (side_ref, both_ref))):
        for pair in range(2):
            low = slice(pair * PAIR, (pair + 1) * PAIR)
            near, far = near_ref[:, low].astype(F32), far_ref[:, low].astype(F32)
            one, two = jnp.where(lower, near, far), jnp.where(lower, far, near)
            for x in range(2):
                dq_ref[:, columns(side ^ flip, pair, x)] = join(one, two, x).astype(BF16)


def total_kernel(parts_ref, dk_ref, dv_ref):
    one, two = (sum_parts(parts_ref, core) for core in range(2))
    dk_ref[...] = join(one, two, 0).astype(BF16)
    dv_ref[...] = join(one, two, 1).astype(BF16)


def sum_parts(parts_ref, core):
    terms = [parts_ref[at].astype(F32) for at in range(core, parts_ref.shape[0], 2)]
    while len(terms) > 1:
        terms = [a + b for a, b in zip(terms[::2], terms[1::2])]
    return terms[0]


def call(kernel, out, *args, last=pltpu.VMEM, scratch=(), flops=0, transcendentals=0):
    vmem = pl.BlockSpec(memory_space=pltpu.VMEM)
    size = sum(a.size * a.dtype.itemsize for a in args) + sum(2 * math.prod(s) for s in out)
    return pl.pallas_call(
        kernel,
        out_shape=tuple(jax.ShapeDtypeStruct(s, BF16) for s in out),
        in_specs=[vmem] * len(args),
        out_specs=(vmem,) * (len(out) - 1) + (pl.BlockSpec(memory_space=last),),
        scratch_shapes=scratch,
        compiler_params=pltpu.CompilerParams(vmem_limit_bytes=32 * 1024 * 1024),
        cost_estimate=pl.CostEstimate(flops=flops, bytes_accessed=size, transcendentals=transcendentals),
    )(*args)


def members(axes, first):
    sizes = [lax.axis_size(axis) for axis in axes]
    order = []
    for place in itertools.product(*map(range, sizes)):
        index = 0
        for at, start, size in zip(place, first, sizes):
            index = index * size + (at + start) % size
        order.append(index)
    return order


def trade(own, side, both, core):
    side = lax.ppermute(side, "xl", CORE_SWAP)
    both = lax.ppermute(both, ("xl", "core"), BOTH_SWAP)
    core = lax.ppermute(core, "core", CORE_SWAP)
    return own, side, both, core


def shards(queries, keys, values, out_grad):
    rows, model = queries.shape
    held = keys.shape[0]
    width = model // 4
    source_order = members(SOURCE_AXES, SOURCE_FIRST)
    grad_order = members(GRAD_AXES, GRAD_FIRST)
    blocks = len(source_order)
    sources = held * blocks

    (spread,) = call(spread_kernel, [(blocks, held, 2 * width)], jnp.concatenate([keys, values], axis=0))
    kv = lax.all_to_all(spread, SOURCE_AXES, 0, 0, axis_index_groups=[source_order], tiled=True)
    targets = trade(*call(quarter_kernel, [(2, rows, width)] * 4, queries, out_grad))

    pairs = 4 * rows * sources * width // HD
    *dq, dkv = call(
        functools.partial(attention_kernel, source_order, grad_order),
        [(rows, width)] * 4 + [(len(grad_order), held, PAIR)],
        *targets,
        kv,
        last=pl.ANY,
        scratch=[
            pltpu.VMEM((sources, 2 * width), F32),
            pltpu.VMEM((len(grad_order), held, PAIR), BF16),
            pltpu.SemaphoreType.DMA((width // HD,)),
        ],
        flops=20 * HD * pairs,
        transcendentals=pairs,
    )
    parts = lax.all_to_all(dkv, GRAD_AXES, 0, 0, axis_index_groups=[grad_order], tiled=True)
    (query_grad,) = call(assemble_kernel, [(rows, model)], *trade(*dq))
    key_grad, value_grad = call(total_kernel, [(held, PAIR), (held, PAIR)], parts)
    return query_grad, key_grad, value_grad


def solution(mesh):
    fine = Mesh(mesh.devices.reshape(2, 2, 2, 8, 4, 2), AXES)
    return jax.shard_map(
        shards,
        mesh=fine,
        in_specs=(P(AXES, None), P(AXES[3:], None), P(AXES[3:], None), P(AXES, None)),
        out_specs=(P(AXES, None), P(AXES[3:], AXES[:3]), P(AXES[3:], AXES[:3])),
        check_vma=False,
    )
```

time: 73.9 us -> 64.9 us (0.88)
  waiting for transfers between devices: 15.7 us -> 7.64 us
  local copies, waits for them, and re-layouts: 1.39 us -> 0.01 us
    all_to_all x3 -> x2, waiting for transfers between devices: 10.4 us -> 3.12 us  [the longest x1 3.11 us: shards(): lax.all_to_all(dkv, GRAD_AXES, 0, 0, axis_index_groups=[grad_order], tile...]
    unnamed x8 -> x4, local copies, waits for them, and re-layouts: 1.39 us -> 0.01 us
    ppermute x2, starting transfers between devices: 4.95 us -> 3.84 us  [trade(): core = lax.ppermute(core, 'core', CORE_SWAP)]
    ppermute x4, waiting for transfers between devices: 5.31 us -> 4.52 us  [the longest x2 4.51 us: trade(): both = lax.ppermute(both, ('xl', 'core'), BOTH_SWAP)]
    all_to_all x3 -> x2, starting transfers between devices: 34.3 us -> 34.2 us  [the longest x1 19.7 us: shards(): lax.all_to_all(spread, SOURCE_AXES, 0, 0, axis_index_groups=[source_order...]
  transfers between devices with their start and end apart: 9 -> 8, of which waited for: 5 -> 3; matrix products, arithmetic and copies ran while one was open for 0% -> 0% of each run, Pallas kernels for 1% -> 2%
where the time goes in v4:
time: 64.9 us; the launch traced here: 64.4 us
  starting transfers between devices  49.6 us (76%)
  waiting for transfers between devices  7.64 us (12%)
  Pallas kernels  5.68 us (9%)
  between operations  0.75 us (1%)
  other arithmetic  0.73 us (1%)
    all_to_all x1, starting transfers between devices, shards(): lax.all_to_all(spread, SOURCE_AXES, 0, 0, axis_index_groups=[source_order...  19.7 us
    all_to_all x1, starting transfers between devices, shards(): lax.all_to_all(dkv, GRAD_AXES, 0, 0, axis_index_groups=[grad_order], tile...  14.4 us
    ppermute x2, starting transfers between devices, trade(): both = lax.ppermute(both, ('xl', 'core'), BOTH_SWAP)  6.28 us
    pallas_call x5, Pallas kernels, call(): pl.pallas_call(kernel, out_shape=tuple((jax.ShapeDtypeStruct(s, BF16) for...  5.68 us
    ppermute x2, starting transfers between devices, trade(): side = lax.ppermute(side, 'xl', CORE_SWAP)  5.34 us
    ppermute x2, waiting for transfers between devices, trade(): both = lax.ppermute(both, ('xl', 'core'), BOTH_SWAP)  4.51 us
    ppermute x2, starting transfers between devices, trade(): core = lax.ppermute(core, 'core', CORE_SWAP)  3.84 us
    all_to_all x1, waiting for transfers between devices, shards(): lax.all_to_all(dkv, GRAD_AXES, 0, 0, axis_index_groups=[grad_order], tile...  3.11 us
  transfers between devices with their start and end apart: 8, of which 3 were waited for; matrix products, arithmetic and copies ran while one was open for 0% of the time, Pallas kernels for 2%

profile of v4, /device:TPU:1, one launch (start us, length us, event | category | flops | bytes accessed | tf_op | source)
XLA Modules:
  0.0 64.4 jit_solution(6550741965153791893)
XLA Ops:
  0.6 0.7 %pad_maximum_fusion.kv_ref = bf16[8,1024]{1,0:T(8,128)(2,1)S(1)} fusion(bf16[4,1024]{1,0:T(4,128)(2,1)} %param.6, bf16[4,1024]{1,0:T(4,128)(2,1)} %param.5), kind=kLoop, calls=%fused_computation | loop fusion | flops 32768 | bytes 32768 | tf_op jit(solution)/shard_map/concatenate | solution.py:186
  1.4 0.8 %shard_map.68 = bf16[64,4,512]{2,1,0:T(4,128)(2,1)} custom-call(bf16[8,1024]{1,0:T(8,128)(2,1)S(1)} %pad_maximum_fusion.kv_ref), custom_call_target="tpu_custom_call" | custom-call | bytes 278528 | tf_op jit(solution)/shard_map/pallas_call | solution.py:148
  2.2 0.0 copy-start
  2.2 0.0 copy-start.1
  2.2 19.7 %all-to-all-start = ((bf16[64,4,512]{2,1,0:T(4,128)(2,1)}), bf16[64,4,512]{2,1,0:T(4,128)(2,1)S(1)}, u32[]{:S(2)}, u32[]{:S(2)}) async-start(bf16[64,4,512]{2,1,0:T(4,128)(2,1)} %shard_map.68), calls=%async_computation | async-start | bytes 524288 | tf_op jit(solution)/shard_map/all_to_all | solution.py:187
  21.9 0.0 copy-done
  21.9 0.0 copy-done.1
  21.9 0.3 shard_map.67
  22.2 3.1 %collective-permute-start = (bf16[2,128,256]{2,1,0:T(8,128)(2,1)S(1)}, bf16[2,128,256]{2,1,0:T(8,128)(2,1)S(1)}, u32[]{:S(2)}, u32[]{:S(2)}) collective-permute-start(bf16[2,128,256]{2,1,0:T(8,128)(2,1)S(1)} %get-tuple-element.15), channel_id=1, source_target_pairs={{0,128},{128,0},{1,129},{129,1},{2,130},{130,2},{3,131},{131,3},{4... | collective-permute-start | bytes 393224 | tf_op jit(solution)/shard_map/ppermute | solution.py:171
  25.4 2.7 %collective-permute-start.1 = (bf16[2,128,256]{2,1,0:T(8,128)(2,1)S(1)}, bf16[2,128,256]{2,1,0:T(8,128)(2,1)S(1)}, u32[]{:S(2)}, u32[]{:S(2)}) collective-permute-start(bf16[2,128,256]{2,1,0:T(8,128)(2,1)S(1)} %get-tuple-element.16), channel_id=1, source_target_pairs={{0,129},{1,128},{128,1},{129,0},{2,131},{3,130},{130,3},{131,2},{4... | collective-permute-start | bytes 393224 | tf_op jit(solution)/shard_map/ppermute | solution.py:172
  28.1 1.9 %collective-permute-start.2 = (bf16[2,128,256]{2,1,0:T(8,128)(2,1)S(1)}, bf16[2,128,256]{2,1,0:T(8,128)(2,1)S(1)}, u32[]{:S(2)}, u32[]{:S(2)}) collective-permute-start(bf16[2,128,256]{2,1,0:T(8,128)(2,1)S(1)} %get-tuple-element.17), channel_id=1, source_target_pairs={{0,1},{1,0},{2,3},{3,2},{4,5},{5,4},{6,7},{7,6},{8,9},{9,8},{10,11... | collective-permute-start | bytes 393224 | tf_op jit(solution)/shard_map/ppermute | solution.py:173
  30.0 0.0 collective-permute-done.refs_1_
  30.0 3.3 %collective-permute-done.1.refs_2_ = bf16[2,128,256]{2,1,0:T(8,128)(2,1)S(1)} collective-permute-done((bf16[2,128,256]{2,1,0:T(8,128)(2,1)S(1)}, bf16[2,128,256]{2,1,0:T(8,128)(2,1)S(1)}, u32[]{:S(2)}, u32[]{:S(2)}) %collective-permute-start.1) | collective-permute-done | bytes 131104 | tf_op jit(solution)/shard_map/ppermute | solution.py:172
  33.3 0.0 collective-permute-done.2.refs_3_
  33.3 0.0 all-to-all-done.refs_4_
  33.3 3.0 %shard_map.69 = (bf16[128,256]{1,0:T(8,128)(2,1)S(1)}, bf16[128,256]{1,0:T(8,128)(2,1)S(1)}, bf16[128,256]{1,0:T(8,128)(2,1)S(1)}, bf16[128,256]{1,0:T(8,128)(2,1)S(1)}, bf16[256,4,128]{2,1,0:T(4,128)(2,1)}) custom-call(bf16[2,128,256]{2,1,0:T(8,128)(2,1)S(1)} %get-tuple-element.14.refs_0_, bf16[2,128,256]{2,1,0:T(8,128)(2,1)S(1)} %collective-permute-done.refs_1_, ...), custom_call_target="tpu_custom_call" | custom-call | flops 671088640 | bytes 1310720 | tf_op jit(solution)/shard_map/pallas_call | solution.py:148
  36.2 14.4 %all-to-all-start.1 = ((bf16[256,4,128]{2,1,0:T(4,128)(2,1)}), bf16[256,4,128]{2,1,0:T(4,128)(2,1)S(1)}, u32[]{:S(2)}, u32[]{:S(2)}) async-start(bf16[256,4,128]{2,1,0:T(4,128)(2,1)} %get-tuple-element.22), calls=%async_computation.1 | async-start | bytes 524288 | tf_op jit(solution)/shard_map/all_to_all | solution.py:205
  50.7 2.2 %collective-permute-start.3 = (bf16[128,256]{1,0:T(8,128)(2,1)S(1)}, bf16[128,256]{1,0:T(8,128)(2,1)S(1)}, u32[]{:S(2)}, u32[]{:S(2)}) collective-permute-start(bf16[128,256]{1,0:T(8,128)(2,1)S(1)} %get-tuple-element.19), channel_id=1, source_target_pairs={{0,128},{128,0},{1,129},{129,1},{2,130},{130,2},{3,131},{131,3},{4... | collective-permute-start | bytes 196616 | tf_op jit(solution)/shard_map/ppermute | solution.py:171
  52.9 3.6 %collective-permute-start.4 = (bf16[128,256]{1,0:T(8,128)(2,1)S(1)}, bf16[128,256]{1,0:T(8,128)(2,1)S(1)}, u32[]{:S(2)}, u32[]{:S(2)}) collective-permute-start(bf16[128,256]{1,0:T(8,128)(2,1)S(1)} %get-tuple-element.20), channel_id=1, source_target_pairs={{0,129},{1,128},{128,1},{129,0},{2,131},{3,130},{130,3},{131,2},{4... | collective-permute-start | bytes 196616 | tf_op jit(solution)/shard_map/ppermute | solution.py:172
  56.5 1.9 %collective-permute-start.5 = (bf16[128,256]{1,0:T(8,128)(2,1)S(1)}, bf16[128,256]{1,0:T(8,128)(2,1)S(1)}, u32[]{:S(2)}, u32[]{:S(2)}) collective-permute-start(bf16[128,256]{1,0:T(8,128)(2,1)S(1)} %get-tuple-element.21), channel_id=1, source_target_pairs={{0,1},{1,0},{2,3},{3,2},{4,5},{5,4},{6,7},{7,6},{8,9},{9,8},{10,11... | collective-permute-start | bytes 196616 | tf_op jit(solution)/shard_map/ppermute | solution.py:173
  58.4 0.0 collective-permute-done.3.side_ref
  58.4 1.3 %collective-permute-done.4.both_ref = bf16[128,256]{1,0:T(8,128)(2,1)S(1)} collective-permute-done((bf16[128,256]{1,0:T(8,128)(2,1)S(1)}, bf16[128,256]{1,0:T(8,128)(2,1)S(1)}, u32[]{:S(2)}, u32[]{:S(2)}) %collective-permute-start.4) | collective-permute-done | bytes 65568 | tf_op jit(solution)/shard_map/ppermute | solution.py:172
  59.7 0.0 collective-permute-done.5.core_ref
  59.7 0.9 %shard_map.70 = bf16[128,1024]{1,0:T(8,128)(2,1)} custom-call(bf16[128,256]{1,0:T(8,128)(2,1)S(1)} %get-tuple-element.18.own_ref, bf16[128,256]{1,0:T(8,128)(2,1)S(1)} %collective-permute-done.3.side_ref, bf16[128,256]{1,0:T(8,128)(2,1)S(1)} %collective-permute-done.4.both_ref, bf16[128,256]{1,0:T(8,128)(2,1)S(1)} %collective-permute-done.5.core_ref), custom_call_target="tpu_custom_call" | custom-call | bytes 524288 | tf_op jit(solution)/shard_map/pallas_call | solution.py:148
  60.5 3.1 %all-to-all-done.1.parts_ref = bf16[256,4,128]{2,1,0:T(4,128)(2,1)S(1)} async-done(((bf16[256,4,128]{2,1,0:T(4,128)(2,1)}), bf16[256,4,128]{2,1,0:T(4,128)(2,1)S(1)}, u32[]{:S(2)}, u32[]{:S(2)}) %all-to-all-start.1) | async-done | bytes 262176 | tf_op jit(solution)/shard_map/all_to_all | solution.py:205
  63.7 0.7 %shard_map.71 = (bf16[4,128]{1,0:T(4,128)(2,1)}, bf16[4,128]{1,0:T(4,128)(2,1)}) custom-call(bf16[256,4,128]{2,1,0:T(4,128)(2,1)S(1)} %all-to-all-done.1.parts_ref), custom_call_target="tpu_custom_call" | custom-call | bytes 264192 | tf_op jit(solution)/shard_map/pallas_call | solution.py:148
Async XLA Ops:
  2.2 19.7 %copy-start = (bf16[128,1024]{1,0:T(8,128)(2,1)S(1)}, bf16[128,1024]{1,0:T(8,128)(2,1)}, u32[]{:S(2)}) copy-start(bf16[128,1024]{1,0:T(8,128)(2,1)} %q_ref.1) | copy-start | bytes 786436
  2.2 19.7 %copy-start.1 = (bf16[128,1024]{1,0:T(8,128)(2,1)S(1)}, bf16[128,1024]{1,0:T(8,128)(2,1)}, u32[]{:S(2)}) copy-start(bf16[128,1024]{1,0:T(8,128)(2,1)} %do_ref.1) | copy-start | bytes 786436
  2.2 31.1 %all-to-all-start = ((bf16[64,4,512]{2,1,0:T(4,128)(2,1)}), bf16[64,4,512]{2,1,0:T(4,128)(2,1)S(1)}, u32[]{:S(2)}, u32[]{:S(2)}) async-start(bf16[64,4,512]{2,1,0:T(4,128)(2,1)} %shard_map.68), calls=%async_computation | async-start | bytes 524288 | tf_op jit(solution)/shard_map/all_to_all | solution.py:187
  22.2 7.8 %collective-permute-start = (bf16[2,128,256]{2,1,0:T(8,128)(2,1)S(1)}, bf16[2,128,256]{2,1,0:T(8,128)(2,1)S(1)}, u32[]{:S(2)}, u32[]{:S(2)}) collective-permute-start(bf16[2,128,256]{2,1,0:T(8,128)(2,1)S(1)} %get-tuple-element.15), channel_id=1, source_target_pairs={{0,128},{128,0},{1,129},{129,1},{2,130},{130,2},{3,131},{131,3},{4... | collective-permute-start | bytes 393224 | tf_op jit(solution)/shard_map/ppermute | solution.py:171
  25.4 7.9 %collective-permute-start.1 = (bf16[2,128,256]{2,1,0:T(8,128)(2,1)S(1)}, bf16[2,128,256]{2,1,0:T(8,128)(2,1)S(1)}, u32[]{:S(2)}, u32[]{:S(2)}) collective-permute-start(bf16[2,128,256]{2,1,0:T(8,128)(2,1)S(1)} %get-tuple-element.16), channel_id=1, source_target_pairs={{0,129},{1,128},{128,1},{129,0},{2,131},{3,130},{130,3},{131,2},{4... | collective-permute-start | bytes 393224 | tf_op jit(solution)/shard_map/ppermute | solution.py:172
  28.1 5.2 %collective-permute-start.2 = (bf16[2,128,256]{2,1,0:T(8,128)(2,1)S(1)}, bf16[2,128,256]{2,1,0:T(8,128)(2,1)S(1)}, u32[]{:S(2)}, u32[]{:S(2)}) collective-permute-start(bf16[2,128,256]{2,1,0:T(8,128)(2,1)S(1)} %get-tuple-element.17), channel_id=1, source_target_pairs={{0,1},{1,0},{2,3},{3,2},{4,5},{5,4},{6,7},{7,6},{8,9},{9,8},{10,11... | collective-permute-start | bytes 393224 | tf_op jit(solution)/shard_map/ppermute | solution.py:173
  36.2 27.4 %all-to-all-start.1 = ((bf16[256,4,128]{2,1,0:T(4,128)(2,1)}), bf16[256,4,128]{2,1,0:T(4,128)(2,1)S(1)}, u32[]{:S(2)}, u32[]{:S(2)}) async-start(bf16[256,4,128]{2,1,0:T(4,128)(2,1)} %get-tuple-element.22), calls=%async_computation.1 | async-start | bytes 524288 | tf_op jit(solution)/shard_map/all_to_all | solution.py:205
  50.7 7.8 %collective-permute-start.3 = (bf16[128,256]{1,0:T(8,128)(2,1)S(1)}, bf16[128,256]{1,0:T(8,128)(2,1)S(1)}, u32[]{:S(2)}, u32[]{:S(2)}) collective-permute-start(bf16[128,256]{1,0:T(8,128)(2,1)S(1)} %get-tuple-element.19), channel_id=1, source_target_pairs={{0,128},{128,0},{1,129},{129,1},{2,130},{130,2},{3,131},{131,3},{4... | collective-permute-start | bytes 196616 | tf_op jit(solution)/shard_map/ppermute | solution.py:171
  52.9 6.8 %collective-permute-start.4 = (bf16[128,256]{1,0:T(8,128)(2,1)S(1)}, bf16[128,256]{1,0:T(8,128)(2,1)S(1)}, u32[]{:S(2)}, u32[]{:S(2)}) collective-permute-start(bf16[128,256]{1,0:T(8,128)(2,1)S(1)} %get-tuple-element.20), channel_id=1, source_target_pairs={{0,129},{1,128},{128,1},{129,0},{2,131},{3,130},{130,3},{131,2},{4... | collective-permute-start | bytes 196616 | tf_op jit(solution)/shard_map/ppermute | solution.py:172
  56.5 3.2 %collective-permute-start.5 = (bf16[128,256]{1,0:T(8,128)(2,1)S(1)}, bf16[128,256]{1,0:T(8,128)(2,1)S(1)}, u32[]{:S(2)}, u32[]{:S(2)}) collective-permute-start(bf16[128,256]{1,0:T(8,128)(2,1)S(1)} %get-tuple-element.21), channel_id=1, source_target_pairs={{0,1},{1,0},{2,3},{3,2},{4,5},{5,4},{6,7},{7,6},{8,9},{9,8},{10,11... | collective-permute-start | bytes 196616 | tf_op jit(solution)/shard_map/ppermute | solution.py:173

commit v5 on v4

--- a/solution.py
+++ b/solution.py
@@ -4,6 +4,7 @@
 
 import jax
 import jax.numpy as jnp
+import numpy as np
 from jax import lax
 from jax.experimental import pallas as pl
 from jax.experimental.pallas import tpu as pltpu
@@ -18,8 +19,8 @@
 AXES = ("xh", "xl", "ylo", "z", "yhi", "core")
 SOURCE_AXES = ("z", "yhi", "core")
 GRAD_AXES = ("xh", "ylo", "z", "yhi", "core")
-SOURCE_FIRST = (7, 2, 0)
-GRAD_FIRST = (0, 0, 4, 0, 0)
+SOURCE_ORDER = ((7, 0, 1, 2, 3, 4, 5, 6), (2, 3, 0, 1), (0, 1))
+GRAD_ORDER = ((1, 0), (0, 1), (5, 6, 7, 0, 1, 2, 3, 4), (0, 1, 2, 3), (0, 1))
 CORE_SWAP = [(0, 1), (1, 0)]
 BOTH_SWAP = [(0, 3), (1, 2), (2, 1), (3, 0)]
 
@@ -52,7 +53,7 @@
     return join(a, b, 0).astype(ref.dtype), join(a, b, 1).astype(ref.dtype)
 
 
-def spread_kernel(kv_ref, out_ref):
+def spread_kernel(order, kv_ref, out_ref):
     side = lax.axis_index("xl")
     held = out_ref.shape[1]
     pieces = []
@@ -62,8 +63,9 @@
     for core in range(2):
         parts = [piece[core][low : low + held] for low in (0, held) for piece in pieces]
         block = jnp.concatenate(parts, axis=1).astype(BF16)
-        for chip in range(out_ref.shape[0] // 2):
-            out_ref[2 * chip + core] = block
+        for at, member in enumerate(order):
+            if member % 2 == core:
+                out_ref[at] = block
 
 
 def quarter_kernel(q_ref, do_ref, *out_refs):
@@ -78,7 +80,7 @@
 
 
 def attention_kernel(source_order, grad_order, *refs):
-    in_refs, kv_ref, dq_refs, dkv_hbm, flat_ref, dkv_ref, sems = refs[:4], refs[4], refs[5:9], *refs[9:]
+    in_refs, kv_ref, dq_refs, dkv_ref, flat_ref = refs[:4], refs[4], refs[5:9], refs[9], refs[10]
     held = kv_ref.shape[1]
     for at, block in enumerate(source_order):
         flat_ref[block * held : (block + 1) * held, :] = kv_ref[at].astype(F32)
@@ -86,7 +88,6 @@
     blocks = sources // held
     places = {member: at for at, member in enumerate(grad_order)}
     rows = in_refs[0].shape[1]
-    copies = []
     for low in range(0, width, PAIR):
         cols = slice(low, low + PAIR)
         k2 = split_lanes(flat_ref[:, cols].astype(BF16))
@@ -107,15 +108,9 @@
             first = (low // HD + part) * blocks
             for at in range(blocks):
                 dkv_ref[places[first + at]] = both[at * held : (at + 1) * held].astype(BF16)
-            span = pl.ds(places[first] // blocks * blocks, blocks)
-            copy = pltpu.make_async_copy(dkv_ref.at[span], dkv_hbm.at[span], sems.at[low // HD + part])
-            copy.start()
-            copies.append(copy)
         dq_t = (matmul(k2.T, ds_low.reshape(2 * sources, 4 * rows)) * SCALE).astype(BF16)
         for at, dq_ref in enumerate(dq_refs):
             dq_ref[:, cols] = dq_t[:, at * rows : (at + 1) * rows].T
-    for copy in copies:
-        copy.wait()
 
 
 def assemble_kernel(own_ref, side_ref, both_ref, core_ref, dq_ref):
@@ -156,15 +151,9 @@
     )(*args)
 
 
-def members(axes, first):
-    sizes = [lax.axis_size(axis) for axis in axes]
-    order = []
-    for place in itertools.product(*map(range, sizes)):
-        index = 0
-        for at, start, size in zip(place, first, sizes):
-            index = index * size + (at + start) % size
-        order.append(index)
-    return order
+def members(orders):
+    sizes = [len(order) for order in orders]
+    return [int(np.ravel_multi_index(place, sizes)) for place in itertools.product(*orders)]
 
 
 def trade(own, side, both, core):
@@ -174,34 +163,35 @@
     return own, side, both, core
 
 
+def run_attention(source_order, grad_order, *args):
+    _, rows, width = args[0].shape
+    blocks, held, _ = args[-1].shape
+    sources = blocks * held
+    pairs = 4 * rows * sources * width // HD
+    return call(
+        functools.partial(attention_kernel, source_order, grad_order),
+        [(rows, width)] * 4 + [(len(grad_order), held, PAIR)],
+        *args,
+        scratch=[pltpu.VMEM((sources, 2 * width), F32)],
+        flops=20 * HD * pairs,
+        transcendentals=pairs,
+    )
+
+
 def shards(queries, keys, values, out_grad):
     rows, model = queries.shape
     held = keys.shape[0]
     width = model // 4
-    source_order = members(SOURCE_AXES, SOURCE_FIRST)
-    grad_order = members(GRAD_AXES, GRAD_FIRST)
+    source_order = [(z * 4 + y) * 2 + c for y in (2, 3, 0, 1) for z in (7, 0, 1, 2, 3, 4, 5, 6) for c in range(2)]
+    grad_order = members(GRAD_ORDER)
     blocks = len(source_order)
     sources = held * blocks
 
-    (spread,) = call(spread_kernel, [(blocks, held, 2 * width)], jnp.concatenate([keys, values], axis=0))
+    (spread,) = call(functools.partial(spread_kernel, source_order), [(blocks, held, 2 * width)], jnp.concatenate([keys, values], axis=0))
     kv = lax.all_to_all(spread, SOURCE_AXES, 0, 0, axis_index_groups=[source_order], tiled=True)
     targets = trade(*call(quarter_kernel, [(2, rows, width)] * 4, queries, out_grad))
 
-    pairs = 4 * rows * sources * width // HD
-    *dq, dkv = call(
-        functools.partial(attention_kernel, source_order, grad_order),
-        [(rows, width)] * 4 + [(len(grad_order), held, PAIR)],
-        *targets,
-        kv,
-        last=pl.ANY,
-        scratch=[
-            pltpu.VMEM((sources, 2 * width), F32),
-            pltpu.VMEM((len(grad_order), held, PAIR), BF16),
-            pltpu.SemaphoreType.DMA((width // HD,)),
-        ],
-        flops=20 * HD * pairs,
-        transcendentals=pairs,
-    )
+    *dq, dkv = run_attention(source_order, grad_order, *targets, kv)
     parts = lax.all_to_all(dkv, GRAD_AXES, 0, 0, axis_index_groups=[grad_order], tiled=True)
     (query_grad,) = call(assemble_kernel, [(rows, model)], *trade(*dq))
     key_grad, value_grad = call(total_kernel, [(held, PAIR), (held, PAIR)], parts)

time: 64.9 us -> 62.7 us (0.966)
  waiting for transfers between devices: 7.64 us -> 5.52 us
    all_to_all x1, waiting for transfers between devices: 3.11 us -> 0.01 us  [shards(): lax.all_to_all(dkv, GRAD_AXES, 0, 0, axis_index_groups=[grad_order], tile...]
    ppermute x2, waiting for transfers between devices: 4.51 us -> 5.5 us  [trade(): both = lax.ppermute(both, ('xl', 'core'), BOTH_SWAP)]
    ppermute x2, starting transfers between devices: 6.28 us -> 5.43 us  [trade(): both = lax.ppermute(both, ('xl', 'core'), BOTH_SWAP)]
    ppermute x2, starting transfers between devices: 5.34 us -> 6.18 us  [trade(): side = lax.ppermute(side, 'xl', CORE_SWAP)]
  transfers between devices with their start and end apart: 8 -> 8, of which waited for: 3 -> 2; matrix products, arithmetic and copies ran while one was open for 0% -> 0% of each run, Pallas kernels for 2% -> 2%
where the time goes in v5:
time: 62.7 us; the launch traced here: 62.1 us
  starting transfers between devices  49.5 us (79%)
  Pallas kernels  5.68 us (9%)
  waiting for transfers between devices  5.52 us (9%)
  between operations  0.74 us (1%)
  other arithmetic  0.73 us (1%)
    all_to_all x1, starting transfers between devices, shards(): lax.all_to_all(spread, SOURCE_AXES, 0, 0, axis_index_groups=[source_order...  19.9 us
    all_to_all x1, starting transfers between devices, shards(): lax.all_to_all(dkv, GRAD_AXES, 0, 0, axis_index_groups=[grad_order], tile...  14.1 us
    ppermute x2, starting transfers between devices, trade(): side = lax.ppermute(side, 'xl', CORE_SWAP)  6.18 us
    pallas_call x5, Pallas kernels, call(): pl.pallas_call(kernel, out_shape=tuple((jax.ShapeDtypeStruct(s, BF16) for...  5.68 us
    ppermute x2, waiting for transfers between devices, trade(): both = lax.ppermute(both, ('xl', 'core'), BOTH_SWAP)  5.5 us
    ppermute x2, starting transfers between devices, trade(): both = lax.ppermute(both, ('xl', 'core'), BOTH_SWAP)  5.43 us
    ppermute x2, starting transfers between devices, trade(): core = lax.ppermute(core, 'core', CORE_SWAP)  3.84 us
  transfers between devices with their start and end apart: 8, of which 2 were waited for; matrix products, arithmetic and copies ran while one was open for 0% of the time, Pallas kernels for 2%

profile of v5, /device:TPU:1, one launch (start us, length us, event | category | flops | bytes accessed | tf_op | source)
XLA Modules:
  0.0 62.1 jit_solution(8244100379553271791)
XLA Ops:
  0.6 0.7 %pad_maximum_fusion.kv_ref = bf16[8,1024]{1,0:T(8,128)(2,1)S(1)} fusion(bf16[4,1024]{1,0:T(4,128)(2,1)} %param.6, bf16[4,1024]{1,0:T(4,128)(2,1)} %param.5), kind=kLoop, calls=%fused_computation | loop fusion | flops 32768 | bytes 32768 | tf_op jit(solution)/shard_map/concatenate | solution.py:190
  1.4 0.8 %shard_map.68 = bf16[64,4,512]{2,1,0:T(4,128)(2,1)} custom-call(bf16[8,1024]{1,0:T(8,128)(2,1)S(1)} %pad_maximum_fusion.kv_ref), custom_call_target="tpu_custom_call" | custom-call | bytes 278528 | tf_op jit(solution)/shard_map/pallas_call | solution.py:143
  2.2 0.0 copy-start
  2.2 0.0 copy-start.1
  2.2 19.9 %all-to-all-start = ((bf16[64,4,512]{2,1,0:T(4,128)(2,1)}), bf16[64,4,512]{2,1,0:T(4,128)(2,1)S(1)}, u32[]{:S(2)}, u32[]{:S(2)}) async-start(bf16[64,4,512]{2,1,0:T(4,128)(2,1)} %shard_map.68), calls=%async_computation | async-start | bytes 524288 | tf_op jit(solution)/shard_map/all_to_all | solution.py:191
  22.0 0.0 copy-done
  22.1 0.0 copy-done.1
  22.1 0.3 shard_map.67
  22.4 3.1 %collective-permute-start = (bf16[2,128,256]{2,1,0:T(8,128)(2,1)S(1)}, bf16[2,128,256]{2,1,0:T(8,128)(2,1)S(1)}, u32[]{:S(2)}, u32[]{:S(2)}) collective-permute-start(bf16[2,128,256]{2,1,0:T(8,128)(2,1)S(1)} %get-tuple-element.15), channel_id=1, source_target_pairs={{0,128},{128,0},{1,129},{129,1},{2,130},{130,2},{3,131},{131,3},{4... | collective-permute-start | bytes 393224 | tf_op jit(solution)/shard_map/ppermute | solution.py:160
  25.5 2.7 %collective-permute-start.1 = (bf16[2,128,256]{2,1,0:T(8,128)(2,1)S(1)}, bf16[2,128,256]{2,1,0:T(8,128)(2,1)S(1)}, u32[]{:S(2)}, u32[]{:S(2)}) collective-permute-start(bf16[2,128,256]{2,1,0:T(8,128)(2,1)S(1)} %get-tuple-element.16), channel_id=1, source_target_pairs={{0,129},{1,128},{128,1},{129,0},{2,131},{3,130},{130,3},{131,2},{4... | collective-permute-start | bytes 393224 | tf_op jit(solution)/shard_map/ppermute | solution.py:161
  28.2 1.9 %collective-permute-start.2 = (bf16[2,128,256]{2,1,0:T(8,128)(2,1)S(1)}, bf16[2,128,256]{2,1,0:T(8,128)(2,1)S(1)}, u32[]{:S(2)}, u32[]{:S(2)}) collective-permute-start(bf16[2,128,256]{2,1,0:T(8,128)(2,1)S(1)} %get-tuple-element.17), channel_id=1, source_target_pairs={{0,1},{1,0},{2,3},{3,2},{4,5},{5,4},{6,7},{7,6},{8,9},{9,8},{10,11... | collective-permute-start | bytes 393224 | tf_op jit(solution)/shard_map/ppermute | solution.py:162
  30.1 0.0 collective-permute-done.refs_1_
  30.1 3.3 %collective-permute-done.1.refs_2_ = bf16[2,128,256]{2,1,0:T(8,128)(2,1)S(1)} collective-permute-done((bf16[2,128,256]{2,1,0:T(8,128)(2,1)S(1)}, bf16[2,128,256]{2,1,0:T(8,128)(2,1)S(1)}, u32[]{:S(2)}, u32[]{:S(2)}) %collective-permute-start.1) | collective-permute-done | bytes 131104 | tf_op jit(solution)/shard_map/ppermute | solution.py:161
  33.4 0.0 collective-permute-done.2.refs_3_
  33.4 0.0 all-to-all-done.refs_4_
  33.4 3.0 %shard_map.69 = (bf16[128,256]{1,0:T(8,128)(2,1)S(1)}, bf16[128,256]{1,0:T(8,128)(2,1)S(1)}, bf16[128,256]{1,0:T(8,128)(2,1)S(1)}, bf16[128,256]{1,0:T(8,128)(2,1)S(1)}, bf16[256,4,128]{2,1,0:T(4,128)(2,1)}) custom-call(bf16[2,128,256]{2,1,0:T(8,128)(2,1)S(1)} %get-tuple-element.14.refs_0_, bf16[2,128,256]{2,1,0:T(8,128)(2,1)S(1)} %collective-permute-done.refs_1_, ...), custom_call_target="tpu_custom_call" | custom-call | flops 671088640 | bytes 1310720 | tf_op jit(solution)/shard_map/pallas_call | solution.py:143
  36.4 14.1 %all-to-all-start.1 = ((bf16[256,4,128]{2,1,0:T(4,128)(2,1)}), bf16[256,4,128]{2,1,0:T(4,128)(2,1)S(1)}, u32[]{:S(2)}, u32[]{:S(2)}) async-start(bf16[256,4,128]{2,1,0:T(4,128)(2,1)} %get-tuple-element.22), calls=%async_computation.1 | async-start | bytes 524288 | tf_op jit(solution)/shard_map/all_to_all | solution.py:195
  50.5 3.1 %collective-permute-start.3 = (bf16[128,256]{1,0:T(8,128)(2,1)S(1)}, bf16[128,256]{1,0:T(8,128)(2,1)S(1)}, u32[]{:S(2)}, u32[]{:S(2)}) collective-permute-start(bf16[128,256]{1,0:T(8,128)(2,1)S(1)} %get-tuple-element.19), channel_id=1, source_target_pairs={{0,128},{128,0},{1,129},{129,1},{2,130},{130,2},{3,131},{131,3},{4... | collective-permute-start | bytes 196616 | tf_op jit(solution)/shard_map/ppermute | solution.py:160
  53.6 2.7 %collective-permute-start.4 = (bf16[128,256]{1,0:T(8,128)(2,1)S(1)}, bf16[128,256]{1,0:T(8,128)(2,1)S(1)}, u32[]{:S(2)}, u32[]{:S(2)}) collective-permute-start(bf16[128,256]{1,0:T(8,128)(2,1)S(1)} %get-tuple-element.20), channel_id=1, source_target_pairs={{0,129},{1,128},{128,1},{129,0},{2,131},{3,130},{130,3},{131,2},{4... | collective-permute-start | bytes 196616 | tf_op jit(solution)/shard_map/ppermute | solution.py:161
  56.3 1.9 %collective-permute-start.5 = (bf16[128,256]{1,0:T(8,128)(2,1)S(1)}, bf16[128,256]{1,0:T(8,128)(2,1)S(1)}, u32[]{:S(2)}, u32[]{:S(2)}) collective-permute-start(bf16[128,256]{1,0:T(8,128)(2,1)S(1)} %get-tuple-element.21), channel_id=1, source_target_pairs={{0,1},{1,0},{2,3},{3,2},{4,5},{5,4},{6,7},{7,6},{8,9},{9,8},{10,11... | collective-permute-start | bytes 196616 | tf_op jit(solution)/shard_map/ppermute | solution.py:162
  58.3 0.0 collective-permute-done.3.side_ref
  58.3 2.2 %collective-permute-done.4.both_ref = bf16[128,256]{1,0:T(8,128)(2,1)S(1)} collective-permute-done((bf16[128,256]{1,0:T(8,128)(2,1)S(1)}, bf16[128,256]{1,0:T(8,128)(2,1)S(1)}, u32[]{:S(2)}, u32[]{:S(2)}) %collective-permute-start.4) | collective-permute-done | bytes 65568 | tf_op jit(solution)/shard_map/ppermute | solution.py:161
  60.5 0.0 collective-permute-done.5.core_ref
  60.5 0.9 %shard_map.70 = bf16[128,1024]{1,0:T(8,128)(2,1)} custom-call(bf16[128,256]{1,0:T(8,128)(2,1)S(1)} %get-tuple-element.18.own_ref, bf16[128,256]{1,0:T(8,128)(2,1)S(1)} %collective-permute-done.3.side_ref, bf16[128,256]{1,0:T(8,128)(2,1)S(1)} %collective-permute-done.4.both_ref, bf16[128,256]{1,0:T(8,128)(2,1)S(1)} %collective-permute-done.5.core_ref), custom_call_target="tpu_custom_call" | custom-call | bytes 524288 | tf_op jit(solution)/shard_map/pallas_call | solution.py:143
  61.4 0.0 all-to-all-done.1.parts_ref
  61.4 0.7 %shard_map.71 = (bf16[4,128]{1,0:T(4,128)(2,1)}, bf16[4,128]{1,0:T(4,128)(2,1)}) custom-call(bf16[256,4,128]{2,1,0:T(4,128)(2,1)S(1)} %all-to-all-done.1.parts_ref), custom_call_target="tpu_custom_call" | custom-call | bytes 264192 | tf_op jit(solution)/shard_map/pallas_call | solution.py:143
Async XLA Ops:
  2.2 19.9 %copy-start = (bf16[128,1024]{1,0:T(8,128)(2,1)S(1)}, bf16[128,1024]{1,0:T(8,128)(2,1)}, u32[]{:S(2)}) copy-start(bf16[128,1024]{1,0:T(8,128)(2,1)} %q_ref.1) | copy-start | bytes 786436
  2.2 19.9 %copy-start.1 = (bf16[128,1024]{1,0:T(8,128)(2,1)S(1)}, bf16[128,1024]{1,0:T(8,128)(2,1)}, u32[]{:S(2)}) copy-start(bf16[128,1024]{1,0:T(8,128)(2,1)} %do_ref.1) | copy-start | bytes 786436
  2.2 31.2 %all-to-all-start = ((bf16[64,4,512]{2,1,0:T(4,128)(2,1)}), bf16[64,4,512]{2,1,0:T(4,128)(2,1)S(1)}, u32[]{:S(2)}, u32[]{:S(2)}) async-start(bf16[64,4,512]{2,1,0:T(4,128)(2,1)} %shard_map.68), calls=%async_computation | async-start | bytes 524288 | tf_op jit(solution)/shard_map/all_to_all | solution.py:191
  22.4 7.8 %collective-permute-start = (bf16[2,128,256]{2,1,0:T(8,128)(2,1)S(1)}, bf16[2,128,256]{2,1,0:T(8,128)(2,1)S(1)}, u32[]{:S(2)}, u32[]{:S(2)}) collective-permute-start(bf16[2,128,256]{2,1,0:T(8,128)(2,1)S(1)} %get-tuple-element.15), channel_id=1, source_target_pairs={{0,128},{128,0},{1,129},{129,1},{2,130},{130,2},{3,131},{131,3},{4... | collective-permute-start | bytes 393224 | tf_op jit(solution)/shard_map/ppermute | solution.py:160
  25.5 7.9 %collective-permute-start.1 = (bf16[2,128,256]{2,1,0:T(8,128)(2,1)S(1)}, bf16[2,128,256]{2,1,0:T(8,128)(2,1)S(1)}, u32[]{:S(2)}, u32[]{:S(2)}) collective-permute-start(bf16[2,128,256]{2,1,0:T(8,128)(2,1)S(1)} %get-tuple-element.16), channel_id=1, source_target_pairs={{0,129},{1,128},{128,1},{129,0},{2,131},{3,130},{130,3},{131,2},{4... | collective-permute-start | bytes 393224 | tf_op jit(solution)/shard_map/ppermute | solution.py:161
  28.2 5.2 %collective-permute-start.2 = (bf16[2,128,256]{2,1,0:T(8,128)(2,1)S(1)}, bf16[2,128,256]{2,1,0:T(8,128)(2,1)S(1)}, u32[]{:S(2)}, u32[]{:S(2)}) collective-permute-start(bf16[2,128,256]{2,1,0:T(8,128)(2,1)S(1)} %get-tuple-element.17), channel_id=1, source_target_pairs={{0,1},{1,0},{2,3},{3,2},{4,5},{5,4},{6,7},{7,6},{8,9},{9,8},{10,11... | collective-permute-start | bytes 393224 | tf_op jit(solution)/shard_map/ppermute | solution.py:162
  36.4 25.0 %all-to-all-start.1 = ((bf16[256,4,128]{2,1,0:T(4,128)(2,1)}), bf16[256,4,128]{2,1,0:T(4,128)(2,1)S(1)}, u32[]{:S(2)}, u32[]{:S(2)}) async-start(bf16[256,4,128]{2,1,0:T(4,128)(2,1)} %get-tuple-element.22), calls=%async_computation.1 | async-start | bytes 524288 | tf_op jit(solution)/shard_map/all_to_all | solution.py:195
  50.5 7.8 %collective-permute-start.3 = (bf16[128,256]{1,0:T(8,128)(2,1)S(1)}, bf16[128,256]{1,0:T(8,128)(2,1)S(1)}, u32[]{:S(2)}, u32[]{:S(2)}) collective-permute-start(bf16[128,256]{1,0:T(8,128)(2,1)S(1)} %get-tuple-element.19), channel_id=1, source_target_pairs={{0,128},{128,0},{1,129},{129,1},{2,130},{130,2},{3,131},{131,3},{4... | collective-permute-start | bytes 196616 | tf_op jit(solution)/shard_map/ppermute | solution.py:160
  53.6 6.9 %collective-permute-start.4 = (bf16[128,256]{1,0:T(8,128)(2,1)S(1)}, bf16[128,256]{1,0:T(8,128)(2,1)S(1)}, u32[]{:S(2)}, u32[]{:S(2)}) collective-permute-start(bf16[128,256]{1,0:T(8,128)(2,1)S(1)} %get-tuple-element.20), channel_id=1, source_target_pairs={{0,129},{1,128},{128,1},{129,0},{2,131},{3,130},{130,3},{131,2},{4... | collective-permute-start | bytes 196616 | tf_op jit(solution)/shard_map/ppermute | solution.py:161
  56.3 4.2 %collective-permute-start.5 = (bf16[128,256]{1,0:T(8,128)(2,1)S(1)}, bf16[128,256]{1,0:T(8,128)(2,1)S(1)}, u32[]{:S(2)}, u32[]{:S(2)}) collective-permute-start(bf16[128,256]{1,0:T(8,128)(2,1)S(1)} %get-tuple-element.21), channel_id=1, source_target_pairs={{0,1},{1,0},{2,3},{3,2},{4,5},{5,4},{6,7},{7,6},{8,9},{9,8},{10,11... | collective-permute-start | bytes 196616 | tf_op jit(solution)/shard_map/ppermute | solution.py:162

commit v6 on v5

--- a/solution.py
+++ b/solution.py
@@ -182,7 +182,7 @@
     rows, model = queries.shape
     held = keys.shape[0]
     width = model // 4
-    source_order = [(z * 4 + y) * 2 + c for y in (2, 3, 0, 1) for z in (7, 0, 1, 2, 3, 4, 5, 6) for c in range(2)]
+    source_order = [(z * 4 + y) * 2 + c for y in (2, 3, 0, 1) for z in (6, 7, 0, 1, 2, 3, 4, 5) for c in range(2)]
     grad_order = members(GRAD_ORDER)
     blocks = len(source_order)
     sources = held * blocks

time: 62.7 us -> 62.1 us (level)
  no operation moved by 1% of the time
where the time goes in v6:
time: 62.1 us; the launch traced here: 61.6 us
  starting transfers between devices  49 us (79%)
  Pallas kernels  5.68 us (9%)
  waiting for transfers between devices  5.48 us (9%)
  between operations  0.74 us (1%)
  other arithmetic  0.73 us (1%)
    all_to_all x1, starting transfers between devices, shards(): lax.all_to_all(spread, SOURCE_AXES, 0, 0, axis_index_groups=[source_order...  19.9 us
    all_to_all x1, starting transfers between devices, shards(): lax.all_to_all(dkv, GRAD_AXES, 0, 0, axis_index_groups=[grad_order], tile...  13.7 us
    ppermute x2, starting transfers between devices, trade(): side = lax.ppermute(side, 'xl', CORE_SWAP)  6.15 us
    pallas_call x5, Pallas kernels, call(): pl.pallas_call(kernel, out_shape=tuple((jax.ShapeDtypeStruct(s, BF16) for...  5.68 us
    ppermute x2, starting transfers between devices, trade(): both = lax.ppermute(both, ('xl', 'core'), BOTH_SWAP)  5.47 us
    ppermute x2, waiting for transfers between devices, trade(): both = lax.ppermute(both, ('xl', 'core'), BOTH_SWAP)  5.46 us
    ppermute x2, starting transfers between devices, trade(): core = lax.ppermute(core, 'core', CORE_SWAP)  3.84 us
  transfers between devices with their start and end apart: 8, of which 2 were waited for; matrix products, arithmetic and copies ran while one was open for 0% of the time, Pallas kernels for 2%

profile of v6, /device:TPU:1, one launch (start us, length us, event | category | flops | bytes accessed | tf_op | source)
XLA Modules:
  0.0 61.6 jit_solution(16334496082602423680)
XLA Ops:
  0.6 0.7 %pad_maximum_fusion.kv_ref = bf16[8,1024]{1,0:T(8,128)(2,1)S(1)} fusion(bf16[4,1024]{1,0:T(4,128)(2,1)} %param.6, bf16[4,1024]{1,0:T(4,128)(2,1)} %param.5), kind=kLoop, calls=%fused_computation | loop fusion | flops 32768 | bytes 32768 | tf_op jit(solution)/shard_map/concatenate | solution.py:190
  1.4 0.8 %shard_map.68 = bf16[64,4,512]{2,1,0:T(4,128)(2,1)} custom-call(bf16[8,1024]{1,0:T(8,128)(2,1)S(1)} %pad_maximum_fusion.kv_ref), custom_call_target="tpu_custom_call" | custom-call | bytes 278528 | tf_op jit(solution)/shard_map/pallas_call | solution.py:143
  2.2 0.0 copy-start
  2.2 0.0 copy-start.1
  2.2 19.9 %all-to-all-start = ((bf16[64,4,512]{2,1,0:T(4,128)(2,1)}), bf16[64,4,512]{2,1,0:T(4,128)(2,1)S(1)}, u32[]{:S(2)}, u32[]{:S(2)}) async-start(bf16[64,4,512]{2,1,0:T(4,128)(2,1)} %shard_map.68), calls=%async_computation | async-start | bytes 524288 | tf_op jit(solution)/shard_map/all_to_all | solution.py:191
  22.0 0.0 copy-done
  22.1 0.0 copy-done.1
  22.1 0.3 shard_map.67
  22.4 3.1 %collective-permute-start = (bf16[2,128,256]{2,1,0:T(8,128)(2,1)S(1)}, bf16[2,128,256]{2,1,0:T(8,128)(2,1)S(1)}, u32[]{:S(2)}, u32[]{:S(2)}) collective-permute-start(bf16[2,128,256]{2,1,0:T(8,128)(2,1)S(1)} %get-tuple-element.15), channel_id=1, source_target_pairs={{0,128},{128,0},{1,129},{129,1},{2,130},{130,2},{3,131},{131,3},{4... | collective-permute-start | bytes 393224 | tf_op jit(solution)/shard_map/ppermute | solution.py:160
  25.5 2.7 %collective-permute-start.1 = (bf16[2,128,256]{2,1,0:T(8,128)(2,1)S(1)}, bf16[2,128,256]{2,1,0:T(8,128)(2,1)S(1)}, u32[]{:S(2)}, u32[]{:S(2)}) collective-permute-start(bf16[2,128,256]{2,1,0:T(8,128)(2,1)S(1)} %get-tuple-element.16), channel_id=1, source_target_pairs={{0,129},{1,128},{128,1},{129,0},{2,131},{3,130},{130,3},{131,2},{4... | collective-permute-start | bytes 393224 | tf_op jit(solution)/shard_map/ppermute | solution.py:161
  28.2 1.9 %collective-permute-start.2 = (bf16[2,128,256]{2,1,0:T(8,128)(2,1)S(1)}, bf16[2,128,256]{2,1,0:T(8,128)(2,1)S(1)}, u32[]{:S(2)}, u32[]{:S(2)}) collective-permute-start(bf16[2,128,256]{2,1,0:T(8,128)(2,1)S(1)} %get-tuple-element.17), channel_id=1, source_target_pairs={{0,1},{1,0},{2,3},{3,2},{4,5},{5,4},{6,7},{7,6},{8,9},{9,8},{10,11... | collective-permute-start | bytes 393224 | tf_op jit(solution)/shard_map/ppermute | solution.py:162
  30.1 0.0 collective-permute-done.refs_1_
  30.2 3.3 %collective-permute-done.1.refs_2_ = bf16[2,128,256]{2,1,0:T(8,128)(2,1)S(1)} collective-permute-done((bf16[2,128,256]{2,1,0:T(8,128)(2,1)S(1)}, bf16[2,128,256]{2,1,0:T(8,128)(2,1)S(1)}, u32[]{:S(2)}, u32[]{:S(2)}) %collective-permute-start.1) | collective-permute-done | bytes 131104 | tf_op jit(solution)/shard_map/ppermute | solution.py:161
  33.4 0.0 collective-permute-done.2.refs_3_
  33.4 0.0 all-to-all-done.refs_4_
  33.4 3.0 %shard_map.69 = (bf16[128,256]{1,0:T(8,128)(2,1)S(1)}, bf16[128,256]{1,0:T(8,128)(2,1)S(1)}, bf16[128,256]{1,0:T(8,128)(2,1)S(1)}, bf16[128,256]{1,0:T(8,128)(2,1)S(1)}, bf16[256,4,128]{2,1,0:T(4,128)(2,1)}) custom-call(bf16[2,128,256]{2,1,0:T(8,128)(2,1)S(1)} %get-tuple-element.14.refs_0_, bf16[2,128,256]{2,1,0:T(8,128)(2,1)S(1)} %collective-permute-done.refs_1_, ...), custom_call_target="tpu_custom_call" | custom-call | flops 671088640 | bytes 1310720 | tf_op jit(solution)/shard_map/pallas_call | solution.py:143
  36.4 13.7 %all-to-all-start.1 = ((bf16[256,4,128]{2,1,0:T(4,128)(2,1)}), bf16[256,4,128]{2,1,0:T(4,128)(2,1)S(1)}, u32[]{:S(2)}, u32[]{:S(2)}) async-start(bf16[256,4,128]{2,1,0:T(4,128)(2,1)} %get-tuple-element.22), calls=%async_computation.1 | async-start | bytes 524288 | tf_op jit(solution)/shard_map/all_to_all | solution.py:195
  50.0 3.0 %collective-permute-start.3 = (bf16[128,256]{1,0:T(8,128)(2,1)S(1)}, bf16[128,256]{1,0:T(8,128)(2,1)S(1)}, u32[]{:S(2)}, u32[]{:S(2)}) collective-permute-start(bf16[128,256]{1,0:T(8,128)(2,1)S(1)} %get-tuple-element.19), channel_id=1, source_target_pairs={{0,128},{128,0},{1,129},{129,1},{2,130},{130,2},{3,131},{131,3},{4... | collective-permute-start | bytes 196616 | tf_op jit(solution)/shard_map/ppermute | solution.py:160
  53.1 2.8 %collective-permute-start.4 = (bf16[128,256]{1,0:T(8,128)(2,1)S(1)}, bf16[128,256]{1,0:T(8,128)(2,1)S(1)}, u32[]{:S(2)}, u32[]{:S(2)}) collective-permute-start(bf16[128,256]{1,0:T(8,128)(2,1)S(1)} %get-tuple-element.20), channel_id=1, source_target_pairs={{0,129},{1,128},{128,1},{129,0},{2,131},{3,130},{130,3},{131,2},{4... | collective-permute-start | bytes 196616 | tf_op jit(solution)/shard_map/ppermute | solution.py:161
  55.9 1.9 %collective-permute-start.5 = (bf16[128,256]{1,0:T(8,128)(2,1)S(1)}, bf16[128,256]{1,0:T(8,128)(2,1)S(1)}, u32[]{:S(2)}, u32[]{:S(2)}) collective-permute-start(bf16[128,256]{1,0:T(8,128)(2,1)S(1)} %get-tuple-element.21), channel_id=1, source_target_pairs={{0,1},{1,0},{2,3},{3,2},{4,5},{5,4},{6,7},{7,6},{8,9},{9,8},{10,11... | collective-permute-start | bytes 196616 | tf_op jit(solution)/shard_map/ppermute | solution.py:162
  57.8 0.0 collective-permute-done.3.side_ref
  57.8 2.2 %collective-permute-done.4.both_ref = bf16[128,256]{1,0:T(8,128)(2,1)S(1)} collective-permute-done((bf16[128,256]{1,0:T(8,128)(2,1)S(1)}, bf16[128,256]{1,0:T(8,128)(2,1)S(1)}, u32[]{:S(2)}, u32[]{:S(2)}) %collective-permute-start.4) | collective-permute-done | bytes 65568 | tf_op jit(solution)/shard_map/ppermute | solution.py:161
  60.0 0.0 collective-permute-done.5.core_ref
  60.0 0.9 %shard_map.70 = bf16[128,1024]{1,0:T(8,128)(2,1)} custom-call(bf16[128,256]{1,0:T(8,128)(2,1)S(1)} %get-tuple-element.18.own_ref, bf16[128,256]{1,0:T(8,128)(2,1)S(1)} %collective-permute-done.3.side_ref, bf16[128,256]{1,0:T(8,128)(2,1)S(1)} %collective-permute-done.4.both_ref, bf16[128,256]{1,0:T(8,128)(2,1)S(1)} %collective-permute-done.5.core_ref), custom_call_target="tpu_custom_call" | custom-call | bytes 524288 | tf_op jit(solution)/shard_map/pallas_call | solution.py:143
  60.9 0.0 all-to-all-done.1.parts_ref
  60.9 0.7 %shard_map.71 = (bf16[4,128]{1,0:T(4,128)(2,1)}, bf16[4,128]{1,0:T(4,128)(2,1)}) custom-call(bf16[256,4,128]{2,1,0:T(4,128)(2,1)S(1)} %all-to-all-done.1.parts_ref), custom_call_target="tpu_custom_call" | custom-call | bytes 264192 | tf_op jit(solution)/shard_map/pallas_call | solution.py:143
Async XLA Ops:
  2.2 19.9 %copy-start = (bf16[128,1024]{1,0:T(8,128)(2,1)S(1)}, bf16[128,1024]{1,0:T(8,128)(2,1)}, u32[]{:S(2)}) copy-start(bf16[128,1024]{1,0:T(8,128)(2,1)} %q_ref.1) | copy-start | bytes 786436
  2.2 19.9 %copy-start.1 = (bf16[128,1024]{1,0:T(8,128)(2,1)S(1)}, bf16[128,1024]{1,0:T(8,128)(2,1)}, u32[]{:S(2)}) copy-start(bf16[128,1024]{1,0:T(8,128)(2,1)} %do_ref.1) | copy-start | bytes 786436
  2.2 31.2 %all-to-all-start = ((bf16[64,4,512]{2,1,0:T(4,128)(2,1)}), bf16[64,4,512]{2,1,0:T(4,128)(2,1)S(1)}, u32[]{:S(2)}, u32[]{:S(2)}) async-start(bf16[64,4,512]{2,1,0:T(4,128)(2,1)} %shard_map.68), calls=%async_computation | async-start | bytes 524288 | tf_op jit(solution)/shard_map/all_to_all | solution.py:191
  22.4 7.8 %collective-permute-start = (bf16[2,128,256]{2,1,0:T(8,128)(2,1)S(1)}, bf16[2,128,256]{2,1,0:T(8,128)(2,1)S(1)}, u32[]{:S(2)}, u32[]{:S(2)}) collective-permute-start(bf16[2,128,256]{2,1,0:T(8,128)(2,1)S(1)} %get-tuple-element.15), channel_id=1, source_target_pairs={{0,128},{128,0},{1,129},{129,1},{2,130},{130,2},{3,131},{131,3},{4... | collective-permute-start | bytes 393224 | tf_op jit(solution)/shard_map/ppermute | solution.py:160
  25.5 7.9 %collective-permute-start.1 = (bf16[2,128,256]{2,1,0:T(8,128)(2,1)S(1)}, bf16[2,128,256]{2,1,0:T(8,128)(2,1)S(1)}, u32[]{:S(2)}, u32[]{:S(2)}) collective-permute-start(bf16[2,128,256]{2,1,0:T(8,128)(2,1)S(1)} %get-tuple-element.16), channel_id=1, source_target_pairs={{0,129},{1,128},{128,1},{129,0},{2,131},{3,130},{130,3},{131,2},{4... | collective-permute-start | bytes 393224 | tf_op jit(solution)/shard_map/ppermute | solution.py:161
  28.2 5.2 %collective-permute-start.2 = (bf16[2,128,256]{2,1,0:T(8,128)(2,1)S(1)}, bf16[2,128,256]{2,1,0:T(8,128)(2,1)S(1)}, u32[]{:S(2)}, u32[]{:S(2)}) collective-permute-start(bf16[2,128,256]{2,1,0:T(8,128)(2,1)S(1)} %get-tuple-element.17), channel_id=1, source_target_pairs={{0,1},{1,0},{2,3},{3,2},{4,5},{5,4},{6,7},{7,6},{8,9},{9,8},{10,11... | collective-permute-start | bytes 393224 | tf_op jit(solution)/shard_map/ppermute | solution.py:162
  36.4 24.5 %all-to-all-start.1 = ((bf16[256,4,128]{2,1,0:T(4,128)(2,1)}), bf16[256,4,128]{2,1,0:T(4,128)(2,1)S(1)}, u32[]{:S(2)}, u32[]{:S(2)}) async-start(bf16[256,4,128]{2,1,0:T(4,128)(2,1)} %get-tuple-element.22), calls=%async_computation.1 | async-start | bytes 524288 | tf_op jit(solution)/shard_map/all_to_all | solution.py:195
  50.0 7.8 %collective-permute-start.3 = (bf16[128,256]{1,0:T(8,128)(2,1)S(1)}, bf16[128,256]{1,0:T(8,128)(2,1)S(1)}, u32[]{:S(2)}, u32[]{:S(2)}) collective-permute-start(bf16[128,256]{1,0:T(8,128)(2,1)S(1)} %get-tuple-element.19), channel_id=1, source_target_pairs={{0,128},{128,0},{1,129},{129,1},{2,130},{130,2},{3,131},{131,3},{4... | collective-permute-start | bytes 196616 | tf_op jit(solution)/shard_map/ppermute | solution.py:160
  53.1 6.9 %collective-permute-start.4 = (bf16[128,256]{1,0:T(8,128)(2,1)S(1)}, bf16[128,256]{1,0:T(8,128)(2,1)S(1)}, u32[]{:S(2)}, u32[]{:S(2)}) collective-permute-start(bf16[128,256]{1,0:T(8,128)(2,1)S(1)} %get-tuple-element.20), channel_id=1, source_target_pairs={{0,129},{1,128},{128,1},{129,0},{2,131},{3,130},{130,3},{131,2},{4... | collective-permute-start | bytes 196616 | tf_op jit(solution)/shard_map/ppermute | solution.py:161
  55.9 4.2 %collective-permute-start.5 = (bf16[128,256]{1,0:T(8,128)(2,1)S(1)}, bf16[128,256]{1,0:T(8,128)(2,1)S(1)}, u32[]{:S(2)}, u32[]{:S(2)}) collective-permute-start(bf16[128,256]{1,0:T(8,128)(2,1)S(1)} %get-tuple-element.21), channel_id=1, source_target_pairs={{0,1},{1,0},{2,3},{3,2},{4,5},{5,4},{6,7},{7,6},{8,9},{9,8},{10,11... | collective-permute-start | bytes 196616 | tf_op jit(solution)/shard_map/ppermute | solution.py:162

commit v7 on v6

--- a/solution.py
+++ b/solution.py
@@ -113,7 +113,7 @@
             dq_ref[:, cols] = dq_t[:, at * rows : (at + 1) * rows].T
 
 
-def assemble_kernel(own_ref, side_ref, both_ref, core_ref, dq_ref):
+def finish_kernel(own_ref, side_ref, both_ref, core_ref, parts_ref, dq_ref, dk_ref, dv_ref):
     lower, side = lax.axis_index("core") == 0, lax.axis_index("xl")
     for flip, (near_ref, far_ref) in enumerate(((own_ref, core_ref), (side_ref, both_ref))):
         for pair in range(2):
@@ -122,9 +122,6 @@
             one, two = jnp.where(lower, near, far), jnp.where(lower, far, near)
             for x in range(2):
                 dq_ref[:, columns(side ^ flip, pair, x)] = join(one, two, x).astype(BF16)
-
-
-def total_kernel(parts_ref, dk_ref, dv_ref):
     one, two = (sum_parts(parts_ref, core) for core in range(2))
     dk_ref[...] = join(one, two, 0).astype(BF16)
     dv_ref[...] = join(one, two, 1).astype(BF16)
@@ -193,9 +190,7 @@
 
     *dq, dkv = run_attention(source_order, grad_order, *targets, kv)
     parts = lax.all_to_all(dkv, GRAD_AXES, 0, 0, axis_index_groups=[grad_order], tiled=True)
-    (query_grad,) = call(assemble_kernel, [(rows, model)], *trade(*dq))
-    key_grad, value_grad = call(total_kernel, [(held, PAIR), (held, PAIR)], parts)
-    return query_grad, key_grad, value_grad
+    return call(finish_kernel, [(rows, model), (held, PAIR), (held, PAIR)], *trade(*dq), parts)
 
 
 def solution(mesh):

time: 62.1 us -> 62.1 us (level)
  Pallas kernels: 5.68 us -> 5.05 us
    pallas_call x5 -> x4, Pallas kernels: 5.68 us -> 5.05 us  [call(): pl.pallas_call(kernel, out_shape=tuple((jax.ShapeDtypeStruct(s, BF16) for...]
  transfers between devices with their start and end apart: 8 -> 8, of which waited for: 2 -> 3; matrix products, arithmetic and copies ran while one was open for 0% -> 0% of each run, Pallas kernels for 2% -> 1%
where the time goes in v7:
time: 62.1 us; the launch traced here: 61.6 us
  starting transfers between devices  49 us (79%)
  waiting for transfers between devices  6.08 us (10%)
  Pallas kernels  5.05 us (8%)
  between operations  0.74 us (1%)
  other arithmetic  0.73 us (1%)
    all_to_all x1, starting transfers between devices, shards(): lax.all_to_all(spread, SOURCE_AXES, 0, 0, axis_index_groups=[source_order...  19.9 us
    all_to_all x1, starting transfers between devices, shards(): lax.all_to_all(dkv, GRAD_AXES, 0, 0, axis_index_groups=[grad_order], tile...  13.7 us
    ppermute x2, starting transfers between devices, trade(): side = lax.ppermute(side, 'xl', CORE_SWAP)  6.15 us
    ppermute x2, starting transfers between devices, trade(): both = lax.ppermute(both, ('xl', 'core'), BOTH_SWAP)  5.47 us
    ppermute x2, waiting for transfers between devices, trade(): both = lax.ppermute(both, ('xl', 'core'), BOTH_SWAP)  5.46 us
    pallas_call x4, Pallas kernels, call(): pl.pallas_call(kernel, out_shape=tuple((jax.ShapeDtypeStruct(s, BF16) for...  5.05 us
    ppermute x2, starting transfers between devices, trade(): core = lax.ppermute(core, 'core', CORE_SWAP)  3.84 us
  transfers between devices with their start and end apart: 8, of which 3 were waited for; matrix products, arithmetic and copies ran while one was open for 0% of the time, Pallas kernels for 1%

profile of v7, /device:TPU:1, one launch (start us, length us, event | category | flops | bytes accessed | tf_op | source)
XLA Modules:
  0.0 61.6 jit_solution(1085314333850386130)
XLA Ops:
  0.6 0.7 %pad_maximum_fusion.kv_ref = bf16[8,1024]{1,0:T(8,128)(2,1)S(1)} fusion(bf16[4,1024]{1,0:T(4,128)(2,1)} %param.6, bf16[4,1024]{1,0:T(4,128)(2,1)} %param.5), kind=kLoop, calls=%fused_computation | loop fusion | flops 32768 | bytes 32768 | tf_op jit(solution)/shard_map/concatenate | solution.py:187
  1.4 0.8 %shard_map.68 = bf16[64,4,512]{2,1,0:T(4,128)(2,1)} custom-call(bf16[8,1024]{1,0:T(8,128)(2,1)S(1)} %pad_maximum_fusion.kv_ref), custom_call_target="tpu_custom_call" | custom-call | bytes 278528 | tf_op jit(solution)/shard_map/pallas_call | solution.py:140
  2.2 0.0 copy-start
  2.2 0.0 copy-start.1
  2.2 19.9 %all-to-all-start = ((bf16[64,4,512]{2,1,0:T(4,128)(2,1)}), bf16[64,4,512]{2,1,0:T(4,128)(2,1)S(1)}, u32[]{:S(2)}, u32[]{:S(2)}) async-start(bf16[64,4,512]{2,1,0:T(4,128)(2,1)} %shard_map.68), calls=%async_computation | async-start | bytes 524288 | tf_op jit(solution)/shard_map/all_to_all | solution.py:188
  22.0 0.0 copy-done
  22.1 0.0 copy-done.1
  22.1 0.3 shard_map.67
  22.4 3.1 %collective-permute-start = (bf16[2,128,256]{2,1,0:T(8,128)(2,1)S(1)}, bf16[2,128,256]{2,1,0:T(8,128)(2,1)S(1)}, u32[]{:S(2)}, u32[]{:S(2)}) collective-permute-start(bf16[2,128,256]{2,1,0:T(8,128)(2,1)S(1)} %get-tuple-element.13), channel_id=1, source_target_pairs={{0,128},{128,0},{1,129},{129,1},{2,130},{130,2},{3,131},{131,3},{4... | collective-permute-start | bytes 393224 | tf_op jit(solution)/shard_map/ppermute | solution.py:157
  25.5 2.7 %collective-permute-start.1 = (bf16[2,128,256]{2,1,0:T(8,128)(2,1)S(1)}, bf16[2,128,256]{2,1,0:T(8,128)(2,1)S(1)}, u32[]{:S(2)}, u32[]{:S(2)}) collective-permute-start(bf16[2,128,256]{2,1,0:T(8,128)(2,1)S(1)} %get-tuple-element.14), channel_id=1, source_target_pairs={{0,129},{1,128},{128,1},{129,0},{2,131},{3,130},{130,3},{131,2},{4... | collective-permute-start | bytes 393224 | tf_op jit(solution)/shard_map/ppermute | solution.py:158
  28.2 1.9 %collective-permute-start.2 = (bf16[2,128,256]{2,1,0:T(8,128)(2,1)S(1)}, bf16[2,128,256]{2,1,0:T(8,128)(2,1)S(1)}, u32[]{:S(2)}, u32[]{:S(2)}) collective-permute-start(bf16[2,128,256]{2,1,0:T(8,128)(2,1)S(1)} %get-tuple-element.15), channel_id=1, source_target_pairs={{0,1},{1,0},{2,3},{3,2},{4,5},{5,4},{6,7},{7,6},{8,9},{9,8},{10,11... | collective-permute-start | bytes 393224 | tf_op jit(solution)/shard_map/ppermute | solution.py:159
  30.1 0.0 collective-permute-done.refs_1_
  30.2 3.3 %collective-permute-done.1.refs_2_ = bf16[2,128,256]{2,1,0:T(8,128)(2,1)S(1)} collective-permute-done((bf16[2,128,256]{2,1,0:T(8,128)(2,1)S(1)}, bf16[2,128,256]{2,1,0:T(8,128)(2,1)S(1)}, u32[]{:S(2)}, u32[]{:S(2)}) %collective-permute-start.1) | collective-permute-done | bytes 131104 | tf_op jit(solution)/shard_map/ppermute | solution.py:158
  33.4 0.0 collective-permute-done.2.refs_3_
  33.4 0.0 all-to-all-done.refs_4_
  33.4 3.0 %shard_map.69 = (bf16[128,256]{1,0:T(8,128)(2,1)S(1)}, bf16[128,256]{1,0:T(8,128)(2,1)S(1)}, bf16[128,256]{1,0:T(8,128)(2,1)S(1)}, bf16[128,256]{1,0:T(8,128)(2,1)S(1)}, bf16[256,4,128]{2,1,0:T(4,128)(2,1)}) custom-call(bf16[2,128,256]{2,1,0:T(8,128)(2,1)S(1)} %get-tuple-element.12.refs_0_, bf16[2,128,256]{2,1,0:T(8,128)(2,1)S(1)} %collective-permute-done.refs_1_, ...), custom_call_target="tpu_custom_call" | custom-call | flops 671088640 | bytes 1310720 | tf_op jit(solution)/shard_map/pallas_call | solution.py:140
  36.4 13.7 %all-to-all-start.1 = ((bf16[256,4,128]{2,1,0:T(4,128)(2,1)}), bf16[256,4,128]{2,1,0:T(4,128)(2,1)S(1)}, u32[]{:S(2)}, u32[]{:S(2)}) async-start(bf16[256,4,128]{2,1,0:T(4,128)(2,1)} %get-tuple-element.20), calls=%async_computation.1 | async-start | bytes 524288 | tf_op jit(solution)/shard_map/all_to_all | solution.py:192
  50.0 3.0 %collective-permute-start.3 = (bf16[128,256]{1,0:T(8,128)(2,1)S(1)}, bf16[128,256]{1,0:T(8,128)(2,1)S(1)}, u32[]{:S(2)}, u32[]{:S(2)}) collective-permute-start(bf16[128,256]{1,0:T(8,128)(2,1)S(1)} %get-tuple-element.17), channel_id=1, source_target_pairs={{0,128},{128,0},{1,129},{129,1},{2,130},{130,2},{3,131},{131,3},{4... | collective-permute-start | bytes 196616 | tf_op jit(solution)/shard_map/ppermute | solution.py:157
  53.1 2.8 %collective-permute-start.4 = (bf16[128,256]{1,0:T(8,128)(2,1)S(1)}, bf16[128,256]{1,0:T(8,128)(2,1)S(1)}, u32[]{:S(2)}, u32[]{:S(2)}) collective-permute-start(bf16[128,256]{1,0:T(8,128)(2,1)S(1)} %get-tuple-element.18), channel_id=1, source_target_pairs={{0,129},{1,128},{128,1},{129,0},{2,131},{3,130},{130,3},{131,2},{4... | collective-permute-start | bytes 196616 | tf_op jit(solution)/shard_map/ppermute | solution.py:158
  55.9 1.9 %collective-permute-start.5 = (bf16[128,256]{1,0:T(8,128)(2,1)S(1)}, bf16[128,256]{1,0:T(8,128)(2,1)S(1)}, u32[]{:S(2)}, u32[]{:S(2)}) collective-permute-start(bf16[128,256]{1,0:T(8,128)(2,1)S(1)} %get-tuple-element.19), channel_id=1, source_target_pairs={{0,1},{1,0},{2,3},{3,2},{4,5},{5,4},{6,7},{7,6},{8,9},{9,8},{10,11... | collective-permute-start | bytes 196616 | tf_op jit(solution)/shard_map/ppermute | solution.py:159
  57.8 0.0 collective-permute-done.3.side_ref
  57.8 2.2 %collective-permute-done.4.both_ref = bf16[128,256]{1,0:T(8,128)(2,1)S(1)} collective-permute-done((bf16[128,256]{1,0:T(8,128)(2,1)S(1)}, bf16[128,256]{1,0:T(8,128)(2,1)S(1)}, u32[]{:S(2)}, u32[]{:S(2)}) %collective-permute-start.4) | collective-permute-done | bytes 65568 | tf_op jit(solution)/shard_map/ppermute | solution.py:158
  60.0 0.0 collective-permute-done.5.core_ref
  60.0 0.6 all-to-all-done.1.parts_ref
  60.6 1.0 %shard_map.70 = (bf16[128,1024]{1,0:T(8,128)(2,1)}, bf16[4,128]{1,0:T(4,128)(2,1)}, bf16[4,128]{1,0:T(4,128)(2,1)}) custom-call(bf16[128,256]{1,0:T(8,128)(2,1)S(1)} %get-tuple-element.16.own_ref, bf16[128,256]{1,0:T(8,128)(2,1)S(1)} %collective-permute-done.3.side_ref, bf16[128,256]{1,0:T(8,128)(2,1)S(1)} %collective-permute-done.4.both_ref, ...), custom_call_target="tpu_custom_call" | custom-call | bytes 788480 | tf_op jit(solution)/shard_map/pallas_call | solution.py:140
Async XLA Ops:
  2.2 19.9 %copy-start = (bf16[128,1024]{1,0:T(8,128)(2,1)S(1)}, bf16[128,1024]{1,0:T(8,128)(2,1)}, u32[]{:S(2)}) copy-start(bf16[128,1024]{1,0:T(8,128)(2,1)} %q_ref.1) | copy-start | bytes 786436
  2.2 19.9 %copy-start.1 = (bf16[128,1024]{1,0:T(8,128)(2,1)S(1)}, bf16[128,1024]{1,0:T(8,128)(2,1)}, u32[]{:S(2)}) copy-start(bf16[128,1024]{1,0:T(8,128)(2,1)} %do_ref.1) | copy-start | bytes 786436
  2.2 31.2 %all-to-all-start = ((bf16[64,4,512]{2,1,0:T(4,128)(2,1)}), bf16[64,4,512]{2,1,0:T(4,128)(2,1)S(1)}, u32[]{:S(2)}, u32[]{:S(2)}) async-start(bf16[64,4,512]{2,1,0:T(4,128)(2,1)} %shard_map.68), calls=%async_computation | async-start | bytes 524288 | tf_op jit(solution)/shard_map/all_to_all | solution.py:188
  22.4 7.8 %collective-permute-start = (bf16[2,128,256]{2,1,0:T(8,128)(2,1)S(1)}, bf16[2,128,256]{2,1,0:T(8,128)(2,1)S(1)}, u32[]{:S(2)}, u32[]{:S(2)}) collective-permute-start(bf16[2,128,256]{2,1,0:T(8,128)(2,1)S(1)} %get-tuple-element.13), channel_id=1, source_target_pairs={{0,128},{128,0},{1,129},{129,1},{2,130},{130,2},{3,131},{131,3},{4... | collective-permute-start | bytes 393224 | tf_op jit(solution)/shard_map/ppermute | solution.py:157
  25.5 7.9 %collective-permute-start.1 = (bf16[2,128,256]{2,1,0:T(8,128)(2,1)S(1)}, bf16[2,128,256]{2,1,0:T(8,128)(2,1)S(1)}, u32[]{:S(2)}, u32[]{:S(2)}) collective-permute-start(bf16[2,128,256]{2,1,0:T(8,128)(2,1)S(1)} %get-tuple-element.14), channel_id=1, source_target_pairs={{0,129},{1,128},{128,1},{129,0},{2,131},{3,130},{130,3},{131,2},{4... | collective-permute-start | bytes 393224 | tf_op jit(solution)/shard_map/ppermute | solution.py:158
  28.2 5.2 %collective-permute-start.2 = (bf16[2,128,256]{2,1,0:T(8,128)(2,1)S(1)}, bf16[2,128,256]{2,1,0:T(8,128)(2,1)S(1)}, u32[]{:S(2)}, u32[]{:S(2)}) collective-permute-start(bf16[2,128,256]{2,1,0:T(8,128)(2,1)S(1)} %get-tuple-element.15), channel_id=1, source_target_pairs={{0,1},{1,0},{2,3},{3,2},{4,5},{5,4},{6,7},{7,6},{8,9},{9,8},{10,11... | collective-permute-start | bytes 393224 | tf_op jit(solution)/shard_map/ppermute | solution.py:159
  36.4 24.3 %all-to-all-start.1 = ((bf16[256,4,128]{2,1,0:T(4,128)(2,1)}), bf16[256,4,128]{2,1,0:T(4,128)(2,1)S(1)}, u32[]{:S(2)}, u32[]{:S(2)}) async-start(bf16[256,4,128]{2,1,0:T(4,128)(2,1)} %get-tuple-element.20), calls=%async_computation.1 | async-start | bytes 524288 | tf_op jit(solution)/shard_map/all_to_all | solution.py:192
  50.0 7.8 %collective-permute-start.3 = (bf16[128,256]{1,0:T(8,128)(2,1)S(1)}, bf16[128,256]{1,0:T(8,128)(2,1)S(1)}, u32[]{:S(2)}, u32[]{:S(2)}) collective-permute-start(bf16[128,256]{1,0:T(8,128)(2,1)S(1)} %get-tuple-element.17), channel_id=1, source_target_pairs={{0,128},{128,0},{1,129},{129,1},{2,130},{130,2},{3,131},{131,3},{4... | collective-permute-start | bytes 196616 | tf_op jit(solution)/shard_map/ppermute | solution.py:157
  53.1 6.9 %collective-permute-start.4 = (bf16[128,256]{1,0:T(8,128)(2,1)S(1)}, bf16[128,256]{1,0:T(8,128)(2,1)S(1)}, u32[]{:S(2)}, u32[]{:S(2)}) collective-permute-start(bf16[128,256]{1,0:T(8,128)(2,1)S(1)} %get-tuple-element.18), channel_id=1, source_target_pairs={{0,129},{1,128},{128,1},{129,0},{2,131},{3,130},{130,3},{131,2},{4... | collective-permute-start | bytes 196616 | tf_op jit(solution)/shard_map/ppermute | solution.py:158
  55.9 4.2 %collective-permute-start.5 = (bf16[128,256]{1,0:T(8,128)(2,1)S(1)}, bf16[128,256]{1,0:T(8,128)(2,1)S(1)}, u32[]{:S(2)}, u32[]{:S(2)}) collective-permute-start(bf16[128,256]{1,0:T(8,128)(2,1)S(1)} %get-tuple-element.19), channel_id=1, source_target_pairs={{0,1},{1,0},{2,3},{3,2},{4,5},{5,4},{6,7},{7,6},{8,9},{9,8},{10,11... | collective-permute-start | bytes 196616 | tf_op jit(solution)/shard_map/ppermute | solution.py:159
